TPU v7x, 32 devices: a whole 2x2x4 slice. The times are simulated.
32 devices in a mesh: dp: 4 (over x, core), ctx: 4 (over z), expert: 2 (over y).
Axes of the slice: x: 2, y: 2, z: 4, core: 2. Of those that a mesh axis runs over, the one named last changes fastest.
Arguments:
- tokens: bfloat16 [8, 1024, 768], P(('dp', 'expert'), 'ctx'), may hold values from -6 to 6
- cotangent: bfloat16 [8, 1024, 768], P(('dp', 'expert'), 'ctx'), may hold values from -6 to 6
- routes: int32 [8, 1024, 1], P(('dp', 'expert'), 'ctx'), may hold values from 0 to 7
- buckets: int32 [2047], replicated, may hold values from 0 to 31
- gain_attn: float32 [768], replicated, may hold values from 0.5 to 1.5
- w_query: bfloat16 [768, 768], replicated, may hold values from -0.109375 to 0.109375
- w_key: bfloat16 [768, 768], replicated, may hold values from -0.109375 to 0.109375
- w_value: bfloat16 [768, 768], replicated, may hold values from -0.21875 to 0.21875
- w_output: bfloat16 [768, 768], replicated, may hold values from -0.875 to 0.875
- bias_table: float32 [32, 12], replicated, may hold values from -6 to 6
- gain_ffn: float32 [768], replicated, may hold values from 0.5 to 1.5
- w_router: bfloat16 [768, 8], replicated, may hold values from -0.15625 to 0.15625
- w_in: bfloat16 [8, 768, 3072], P(('dp', 'expert'), None, 'ctx'), may hold values from -0.21875 to 0.21875
- w_out: bfloat16 [8, 3072, 768], P(('dp', 'expert'), 'ctx'), may hold values from -0.875 to 0.875
Outputs:
- layer_out: bfloat16 [8, 1024, 768], P(('dp', 'expert'), 'ctx')
- grad_tokens: bfloat16 [8, 1024, 768], P(('dp', 'expert'), 'ctx')
- grad_gain_attn: float32 [768], replicated
- grad_query: float32 [768, 768], replicated
- grad_key: float32 [768, 768], replicated
- grad_value: float32 [768, 768], replicated
- grad_output: float32 [768, 768], replicated
- grad_bias_table: float32 [32, 12], replicated
- grad_gain_ffn: float32 [768], replicated
- grad_router: float32 [768, 8], replicated
- grad_w_in: float32 [8, 768, 3072], P(('dp', 'expert'), None, 'ctx')
- grad_w_out: float32 [8, 3072, 768], P(('dp', 'expert'), 'ctx')
All inputs are finite; a program needn't handle non-finite values.
Results may differ from a plain program's by a relative error of at most 0.018.
Values may be sent and summed in bfloat16 or wider, within the bound.
No kernel may reach another device: no remote copies, remote signals or barrier semaphores. Data moves between devices by JAX's collectives and lax.ppermute only.
A program may use at most 256 MiB of HBM per device.

v0:
```python
import jax
import jax.numpy as jnp
from jax import lax
from jax.sharding import PartitionSpec as P

H = 12
HD = 64
NB = 32


epsilon = 1e-06
exact_prec = lax.Precision.HIGHEST


def norm_scale(row_data):
    return lax.rsqrt(jnp.mean(row_data * row_data, axis=-1, keepdims=True) + epsilon)


def norm_back(grad_in, row_data, scale, gain):
    weighted = grad_in * gain
    inner = jnp.mean(weighted * row_data, axis=-1, keepdims=True)
    return scale * weighted - row_data * (scale * scale * scale) * inner


def smooth_act(values):
    return jax.nn.gelu(values, approximate=False)


def gelu_with_back(pre_act):
    return jax.vjp(smooth_act, pre_act)


def contract_rows(left, right):
    return lax.dot_general(
        left, right, (((0,), (0,)), ((), ())), preferred_element_type=jnp.float32
    )


def offset_start(query_start, query_count, key_start, full_len):
    return key_start - query_start + full_len - query_count


def bias_block(rel_bias, base, query_count, key_count):
    width = query_count + key_count - 1
    segment = lax.dynamic_slice_in_dim(rel_bias, base, width, 1)
    heads = segment.shape[0]
    spread = jnp.broadcast_to(segment[:, None, :], (heads, query_count, width)).reshape(
        heads, query_count * width
    )
    skewed = spread[:, query_count - 1 : query_count - 1 + query_count * (width - 1)]
    return skewed.reshape(heads, query_count, width - 1)[:, :, :key_count]


def bias_grad_block(grad_block, query_count, key_count):
    width = query_count + key_count - 1
    heads = grad_block.shape[0]
    padded = jnp.pad(grad_block, ((0, 0), (0, 0), (0, width - 1 - key_count)))
    flat = padded.reshape(heads, query_count * (width - 1))
    flat = jnp.pad(flat, ((0, 0), (query_count - 1, 1)))
    return jnp.sum(flat.reshape(heads, query_count, width), axis=1)


def shards(
    tokens,
    cotangent,
    routes,
    buckets,
    gain_attn,
    w_query,
    w_key,
    w_value,
    w_output,
    bias_table,
    gain_ffn,
    w_router,
    w_in,
    w_out,
):
    seq_dev, block_len, model_width = tokens.shape
    ctx_size = lax.axis_size("ctx")
    experts = lax.axis_size(("dp", "expert"))
    full_len = block_len * ctx_size
    tok_count = seq_dev * block_len
    capacity = max(2, (5 * tok_count + 4 * experts - 1) // (4 * experts))
    query_start = lax.axis_index("ctx") * block_len
    bfloat = jnp.bfloat16
    single = jnp.float32
    row_data = tokens.reshape(tok_count, model_width).astype(single)
    scale_one = norm_scale(row_data)
    normed_one = (row_data * scale_one * gain_attn).astype(bfloat)
    query_rows = jnp.dot(normed_one, w_query, preferred_element_type=single).astype(bfloat)
    key_rows = jnp.dot(normed_one, w_key, preferred_element_type=single).astype(bfloat)
    value_rows = jnp.dot(normed_one, w_value, preferred_element_type=single).astype(bfloat)
    query_heads = query_rows.reshape(seq_dev, block_len, H, HD)
    key_blocks = key_rows.reshape(seq_dev, block_len, model_width)
    value_blocks = value_rows.reshape(seq_dev, block_len, model_width)
    bucket_hot = (buckets[:, None] == jnp.arange(NB, dtype=jnp.int32)[None, :]).astype(single)
    rel_bias = lax.dot_general(
        bias_table, bucket_hot, (((0,), (1,)), ((), ())), precision=exact_prec
    )
    key_all, value_all = (
        lax.all_gather(key_blocks, "ctx", axis=1, tiled=True),
        lax.all_gather(value_blocks, "ctx", axis=1, tiled=True),
    )
    key_heads_all = key_all.reshape(seq_dev, full_len, H, HD)
    value_heads_all = value_all.reshape(seq_dev, full_len, H, HD)
    base_all = offset_start(query_start, block_len, 0, full_len)
    scores_all = jnp.einsum(
        "sqhd,skhd->shqk", query_heads, key_heads_all, preferred_element_type=single
    )
    scores_all = scores_all + bias_block(rel_bias, base_all, block_len, full_len)[None]
    row_max = jnp.max(scores_all, axis=-1)
    expd = jnp.exp(scores_all - row_max[..., None])
    row_sum = jnp.sum(expd, axis=-1)
    soft_all = expd / row_sum[..., None]
    attn_heads = jnp.einsum(
        "shqk,skhd->sqhd", soft_all.astype(bfloat), value_heads_all, preferred_element_type=single
    )
    attn_exact = jnp.einsum(
        "shqk,skhd->sqhd", soft_all, value_heads_all.astype(single), precision=exact_prec
    )
    attn_rows = attn_heads.reshape(tok_count, model_width).astype(bfloat)
    resid = row_data + jnp.dot(attn_rows, w_output, preferred_element_type=single)
    scale_two = norm_scale(resid)
    normed_two = (resid * scale_two * gain_ffn).astype(bfloat)
    logits = jnp.dot(normed_two, w_router, preferred_element_type=single)
    probs = jax.nn.softmax(logits, axis=-1)
    route_flat = routes.reshape(tok_count)
    route_hot = (route_flat[:, None] == jnp.arange(experts, dtype=jnp.int32)[None, :]).astype(
        jnp.int32
    )
    route_float = route_hot.astype(single)
    gate = jnp.sum(probs * route_float, axis=-1)
    slot_index = jnp.sum((jnp.cumsum(route_hot, axis=0) - route_hot) * route_hot, axis=1)
    target = jnp.where(slot_index < capacity, route_flat * capacity + slot_index, -1)
    dispatch_mat = (
        target[:, None] == jnp.arange(experts * capacity, dtype=jnp.int32)[None, :]
    ).astype(bfloat)
    buffer = (
        contract_rows(dispatch_mat, normed_two)
        .astype(bfloat)
        .reshape(experts, capacity, model_width)
    )
    received = lax.all_to_all(buffer, ("dp", "expert"), split_axis=0, concat_axis=1, tiled=True)
    local_rows = received[0]
    first_full, second_full = (
        lax.all_gather(w_in, "ctx", axis=2, tiled=True),
        lax.all_gather(w_out, "ctx", axis=1, tiled=True),
    )
    first_proj = first_full[0]
    second_proj = second_full[0]
    pre_act = jnp.dot(local_rows, first_proj, preferred_element_type=single)
    hidden_full, act_pull = gelu_with_back(pre_act)
    hidden = hidden_full.astype(bfloat)
    expert_out = jnp.dot(hidden, second_proj, preferred_element_type=single).astype(bfloat)
    returned = lax.all_to_all(
        expert_out[None], ("dp", "expert"), split_axis=1, concat_axis=0, tiled=True
    )
    picked = jnp.dot(
        dispatch_mat,
        returned.reshape(experts * capacity, model_width),
        preferred_element_type=single,
    )
    layer_out = resid + gate[:, None] * picked
    grad_in = cotangent.reshape(tok_count, model_width).astype(single)
    grad_gate = jnp.sum(grad_in * picked, axis=-1)
    grad_picked = (gate[:, None] * grad_in).astype(bfloat)
    grad_buffer = (
        contract_rows(dispatch_mat, grad_picked)
        .astype(bfloat)
        .reshape(experts, capacity, model_width)
    )
    grad_received = lax.all_to_all(
        grad_buffer, ("dp", "expert"), split_axis=0, concat_axis=1, tiled=True
    )
    grad_local = grad_received[0]
    grad_hidden = jnp.dot(grad_local, second_proj.T, preferred_element_type=single)
    grad_pre = act_pull(grad_hidden)[0].astype(bfloat)
    full_second = contract_rows(hidden, grad_local)
    full_first = contract_rows(local_rows, grad_pre)
    grad_first, grad_second = (
        lax.psum_scatter(
            full_first[None].astype(jnp.bfloat16), "ctx", scatter_dimension=2, tiled=True
        ).astype(jnp.float32),
        lax.psum_scatter(
            full_second[None].astype(jnp.bfloat16), "ctx", scatter_dimension=1, tiled=True
        ).astype(jnp.float32),
    )
    grad_rows = jnp.dot(grad_pre, first_proj.T, preferred_element_type=single).astype(bfloat)
    grad_returned = lax.all_to_all(
        grad_rows[None], ("dp", "expert"), split_axis=1, concat_axis=0, tiled=True
    )
    grad_logits = (grad_gate[:, None] * probs * (route_float - gate[:, None])).astype(bfloat)
    grad_router = contract_rows(normed_two, grad_logits)
    grad_normed_two = jnp.dot(
        dispatch_mat,
        grad_returned.reshape(experts * capacity, model_width),
        preferred_element_type=single,
    )
    grad_normed_two = grad_normed_two + jnp.dot(
        grad_logits, w_router.T, preferred_element_type=single
    )
    grad_gain_ffn = jnp.sum(grad_normed_two * resid * scale_two, axis=0)
    grad_resid = grad_in + norm_back(grad_normed_two, resid, scale_two, gain_ffn)
    grad_branch = grad_resid.astype(bfloat)
    grad_output = contract_rows(attn_rows, grad_branch)
    grad_attn = jnp.dot(grad_branch, w_output.T, preferred_element_type=single).astype(bfloat)
    grad_attn_heads = grad_attn.reshape(seq_dev, block_len, H, HD)
    delta_rows = jnp.sum(grad_attn_heads.astype(single) * attn_exact, axis=-1).transpose(0, 2, 1)
    grad_rel = jnp.zeros((H, 2 * full_len - 1), single)
    key_part = lax.all_gather(key_blocks, "ctx", axis=1, tiled=True)
    value_part = lax.all_gather(value_blocks, "ctx", axis=1, tiled=True)
    seg_count = key_part.shape[1]
    key_heads = key_part.reshape(seq_dev, seg_count, H, HD)
    value_heads = value_part.reshape(seq_dev, seg_count, H, HD)
    base = offset_start(query_start, block_len, jnp.int32(0), full_len)
    scores = jnp.einsum("sqhd,skhd->shqk", query_heads, key_heads, preferred_element_type=single)
    scores = scores + bias_block(rel_bias, base, block_len, seg_count)[None]
    soft_weights = jnp.exp(scores - row_max[..., None]) / row_sum[..., None]
    grad_soft = jnp.einsum(
        "sqhd,skhd->shqk", grad_attn_heads, value_heads, preferred_element_type=single
    )
    grad_scores = (soft_weights * (grad_soft - delta_rows[..., None])).astype(bfloat)
    grad_query_acc = jnp.einsum(
        "shqk,skhd->sqhd", grad_scores, key_heads, preferred_element_type=single
    )
    key_term = jnp.einsum(
        "shqk,sqhd->skhd", grad_scores, query_heads, preferred_element_type=single
    ).reshape(seq_dev, seg_count, model_width)
    value_term = jnp.einsum(
        "shqk,sqhd->skhd",
        soft_weights.astype(bfloat),
        grad_attn_heads,
        preferred_element_type=single,
    ).reshape(seq_dev, seg_count, model_width)
    grad_key_all = key_term
    grad_value_all = value_term
    head_scores = jnp.sum(grad_scores.astype(single), axis=0)
    diagonal_sums = bias_grad_block(head_scores, block_len, seg_count)
    grad_rel = lax.dynamic_update_slice_in_dim(grad_rel, diagonal_sums, base, 1)
    grad_query_acc, grad_key_all, grad_value_all, grad_rel = (
        grad_query_acc,
        grad_key_all,
        grad_value_all,
        grad_rel,
    )
    grad_key_own, grad_value_own = (
        lax.psum_scatter(
            grad_key_all.astype(jnp.bfloat16), "ctx", scatter_dimension=1, tiled=True
        ).astype(jnp.float32),
        lax.psum_scatter(
            grad_value_all.astype(jnp.bfloat16), "ctx", scatter_dimension=1, tiled=True
        ).astype(jnp.float32),
    )
    grad_query_rows = grad_query_acc.reshape(tok_count, model_width).astype(bfloat)
    grad_key_rows = grad_key_own.reshape(tok_count, model_width).astype(bfloat)
    grad_value_rows = grad_value_own.reshape(tok_count, model_width).astype(bfloat)
    grad_query_w = contract_rows(normed_one, grad_query_rows)
    grad_key_w = contract_rows(normed_one, grad_key_rows)
    grad_value_w = contract_rows(normed_one, grad_value_rows)
    grad_normed_one = jnp.dot(grad_query_rows, w_query.T, preferred_element_type=single)
    grad_normed_one = grad_normed_one + jnp.dot(
        grad_key_rows, w_key.T, preferred_element_type=single
    )
    grad_normed_one = grad_normed_one + jnp.dot(
        grad_value_rows, w_value.T, preferred_element_type=single
    )
    grad_gain_attn = jnp.sum(grad_normed_one * row_data * scale_one, axis=0)
    grad_tokens = grad_resid + norm_back(grad_normed_one, row_data, scale_one, gain_attn)
    grad_table = lax.dot_general(
        bucket_hot, grad_rel, (((0,), (1,)), ((), ())), precision=exact_prec
    )
    summed = lax.psum(
        (
            grad_gain_attn,
            grad_query_w,
            grad_key_w,
            grad_value_w,
            grad_output,
            grad_table,
            grad_gain_ffn,
            grad_router,
        ),
        ("dp", "ctx", "expert"),
    )
    return (
        layer_out.reshape(seq_dev, block_len, model_width).astype(bfloat),
        grad_tokens.reshape(seq_dev, block_len, model_width).astype(bfloat),
        summed[0],
        summed[1],
        summed[2],
        summed[3],
        summed[4],
        summed[5],
        summed[6],
        summed[7],
        grad_first,
        grad_second,
    )


def solution(mesh):
    placed = (
        P(("dp", "expert"), "ctx", None),
        P(("dp", "expert"), "ctx", None),
        P(("dp", "expert"), "ctx", None),
        P(),
        P(),
        P(),
        P(),
        P(),
        P(),
        P(),
        P(),
        P(),
        P(("dp", "expert"), None, "ctx"),
        P(("dp", "expert"), "ctx", None),
    )
    return jax.shard_map(
        shards,
        mesh=mesh,
        in_specs=placed,
        out_specs=(
            P(("dp", "expert"), "ctx", None),
            P(("dp", "expert"), "ctx", None),
            P(),
            P(),
            P(),
            P(),
            P(),
            P(),
            P(),
            P(),
            P(("dp", "expert"), None, "ctx"),
            P(("dp", "expert"), "ctx", None),
        ),
        check_vma=False,
    )
```

profile of v0, /device:TPU:0, one launch (start us, length us, event | category | flops | bytes accessed | tf_op | source)
XLA Modules:
  0.0 815.8 jit_solution(3193349276353569488)
XLA Ops:
  16.5 6.8 broadcast_in_dim.11
  23.3 25.2 %reshape.336 = f32[12,327424]{1,0:T(8,128)} reshape(f32[12,256,1279]{2,1,0:T(8,128)} %broadcast_in_dim.11) | data formatting | bytes 31432704 | tf_op jit(solution)/shard_map/reshape | solution.py:47
  48.5 17.9 %slice.18 = f32[12,327168]{1,0:T(8,128)} slice(f32[12,327424]{1,0:T(8,128)} %reshape.336), slice={[0:12], [255:327423]} | slice | bytes 31408128 | tf_op jit(solution)/shard_map/slice | solution.py:50
  66.5 32.1 %reshape.337 = f32[12,256,1278]{2,1,0:T(8,128)} reshape(f32[12,327168]{1,0:T(8,128)} %slice.18) | data formatting | bytes 31408128 | tf_op jit(solution)/shard_map/reshape | solution.py:51
  103.3 9.1 %fusion.113 = (f32[12,256]{1,0:T(8,128)}, f32[12,256,1024]{2,1,0:T(8,128)}) fusion(f32[12,256,1278]{2,1,0:T(8,128)} %reshape.337, bf16[256,12,64]{0,2,1:T(8,128)(2,1)S(1)} %bitcast.205, bf16[1024,12,64]{0,2,1:T(8,128)(2,1)S(1)} %bitcast.202), kind=kOutput, calls=%fused_computation.144 | convolution fusion | flops 408941568 | bytes 27144192 | tf_op jit(solution)/shard_map/sqhd,skhd->shqk/dot_general | solution.py:108
  115.0 7.7 fusion.1
  123.4 4.2 fusion.34
  130.6 5.1 all-to-all-start
  144.3 4.1 all-to-all-start.2
  148.4 31.3 %all-gather.7.cloned.1.call-done = bf16[1,768,3072]{2,1,0:T(8,128)(2,1)} async-done(((bf16[1,768,768]{2,1,0:T(8,128)(2,1)}), bf16[1,768,3072]{2,1,0:T(8,128)(2,1)}) %all-gather.7.cloned.1.call-update) | async-done | bytes 4718608 | tf_op jit(solution)/shard_map/all_gather | solution.py:147
  179.8 13.6 %multiply_convert_fusion.1 = (bf16[320,3072]{1,0:T(8,128)(2,1)}, f32[320,3072]{1,0:T(8,128)}, f32[320,3072]{1,0:T(8,128)}) fusion(bf16[320,768]{1,0:T(8,128)(2,1)} %bitcast.13, bf16[1,768,3072]{2,1,0:T(8,128)(2,1)} %all-gather.7.cloned.1.call-done), kind=kOutput, calls=%fused_computation.21 | convolution fusion | flops 1573847040 | bytes 15040512 | tf_op jit(solution)/shard_map/dot_general | solution.py:152
  193.4 75.7 %all-gather.9.cloned.1.call-done = bf16[1,3072,768]{2,1,0:T(8,128)(2,1)} async-done(((bf16[1,768,768]{2,1,0:T(8,128)(2,1)}), bf16[1,3072,768]{2,1,0:T(8,128)(2,1)}) %all-gather.9.cloned.1.call-update) | async-done | bytes 4718608 | tf_op jit(solution)/shard_map/all_gather | solution.py:148
  269.0 7.5 add_convert_fusion
  280.5 5.3 reduce.7
  287.8 4.1 all-to-all-start.3
  291.9 4.6 fusion.37
  298.3 5.3 reduce.8
  334.1 12.5 %fusion.43 = f32[256,12]{0,1:T(8,128)S(1)} fusion(f32[1,256,12,64]{1,3,2,0:T(8,128)} %bitcast.221, bf16[1024,12,64]{0,2,1:T(8,128)(2,1)} %bitcast.218, f32[12,256,1024]{2,1,0:T(8,128)} %get-tuple-element.33, f32[12,256]{1,0:T(8,128)} %copy-done.40, f32[12,256]{1,0:T(8,128)} %get-tuple-element.32), kind=kOutput, calls=%fused_computation.59 | convolution fusion | flops 2422600704 | bytes 14979072 | tf_op jit(solution)/shard_map/shqk,skhd->sqhd/dot_general | solution.py:119
  346.6 7.0 multiply_convert_fusion
  356.9 8.0 fusion.24
  365.1 6.5 fusion.10
  371.6 6.4 fusion.11
  378.1 6.7 pad.10
  384.8 24.5 %reshape.344 = bf16[12,327168]{1,0:T(8,128)(2,1)} reshape(bf16[12,256,1278]{2,1,0:T(8,128)(2,1)} %pad.10) | data formatting | bytes 15704064 | tf_op jit(solution)/shard_map/reshape | solution.py:58
  409.3 4.9 convolution_convert_fusion.5
  421.9 4.9 reduce-scatter.7.cloned.1.call-done
  429.8 12.6 %pad_convert_fusion = f32[12,327424]{1,0:T(8,128)} fusion(bf16[12,327168]{1,0:T(8,128)(2,1)} %reshape.344), kind=kLoop, calls=%fused_computation.5 | loop fusion | flops 3929088 | bytes 23568384 | tf_op jit(solution)/shard_map/reshape | solution.py:60
  442.4 31.2 %reshape.351 = f32[12,256,1279]{2,1,0:T(8,128)} reshape(f32[12,327424]{1,0:T(8,128)} %pad_convert_fusion) | data formatting | bytes 31432704 | tf_op jit(solution)/shard_map/reshape | solution.py:60
  473.8 6.4 reduce_sum.135
  488.3 44.1 %all-reduce.2 = (f32[768]{0:T(1024)}, f32[32,12]{0,1:T(8,128)}, f32[768]{0:T(1024)}, f32[768,8]{0,1:T(8,128)}) all-reduce(f32[768]{0:T(1024)S(1)} %get-tuple-element.14, f32[32,12]{0,1:T(8,128)S(1)} %copy-done.46, f32[768]{0:T(1024)S(1)} %copy-done.42, ...), channel_id=1, replica_groups=mesh['dp'=4,'ctx'=4,'expert'=2] {'dp','ctx','expert'}, use_global_device_ids=true, to_apply=%region_17.18 | all-reduce | flops 8064 | bytes 64512 | tf_op jit(solution)/shard_map/psum | solution.py:273
  536.2 65.9 %reduce-scatter.11.cloned.1.call-done = bf16[1,768,768]{2,1,0:T(8,128)(2,1)} async-done(((bf16[1,3072,768]{2,1,0:T(8,128)(2,1)}), bf16[1,768,768]{2,1,0:T(8,128)(2,1)}) %reduce-scatter.11.cloned.1.call-update) | async-done | bytes 1179664 | tf_op jit(solution)/shard_map/reduce_scatter | solution.py:185
  605.0 196.4 %all-reduce.6.cloned.1.call-done = (f32[768,768]{1,0:T(8,128)}, f32[768,768]{1,0:T(8,128)}, f32[768,768]{1,0:T(8,128)}, f32[768,768]{1,0:T(8,128)}) async-done(((f32[768,768]{1,0:T(8,128)}, f32[768,768]{1,0:T(8,128)}, f32[768,768]{1,0:T(8,128)}, f32[768,768]{1,0:T(8,128)}), (f32[768,768]{1,0:T(8,128)}, f32[768,768]{1,0:T(8,128)}, f32[768,768]{1,0:T(8,128)}, ...) | async-done | bytes 9437200 | tf_op jit(solution)/shard_map/psum | solution.py:273
  (194 shorter events, 103.2 us)
Async XLA Ops:
  7.2 94.4 %all-gather.13.cloned.1.call-start = ((), (), s32[]{:S(2)}) async-start(), calls=%async_computation.15 | async-start | bytes 1966080 | tf_op jit(solution)/shard_map/all_gather | solution.py:102
  11.8 100.6 %all-gather.11.cloned.1.call-start = ((), (), s32[]{:S(2)}) async-start(), calls=%async_computation.14 | async-start | bytes 1966080 | tf_op jit(solution)/shard_map/all_gather | solution.py:103
  14.2 165.6 %all-gather.7.cloned.1.call-start = ((), (), s32[]{:S(2)}) async-start(), calls=%async_computation.8 | async-start | bytes 5898240 | tf_op jit(solution)/shard_map/all_gather | solution.py:147
  14.9 254.2 %all-gather.9.cloned.1.call-start = ((), (), s32[]{:S(2)}) async-start(), calls=%async_computation.9 | async-start | bytes 5898240 | tf_op jit(solution)/shard_map/all_gather | solution.py:148
  66.4 32.1 %copy-start.3 = (bf16[1,256,768]{2,1,0:T(8,128)(2,1)S(1)}, bf16[1,256,768]{2,1,0:T(8,128)(2,1)}, u32[]{:S(2)}) copy-start(bf16[1,256,768]{2,1,0:T(8,128)(2,1)} %param.14) | copy-start | bytes 1179652
  66.5 32.1 %copy-start.23 = (bf16[768,768]{1,0:T(8,128)(2,1)S(1)}, bf16[768,768]{1,0:T(8,128)(2,1)}, u32[]{:S(2)}) copy-start(bf16[768,768]{1,0:T(8,128)(2,1)} %param.19) | copy-start | bytes 3538948
  66.5 32.1 %copy-start.25 = (f32[768]{0:T(1024)S(1)}, f32[768]{0:T(1024)}, u32[]{:S(2)}) copy-start(f32[768]{0:T(1024)} %param.18) | copy-start | bytes 9220
  66.5 32.8 %copy-start.29 = (s32[1,256,1]{1,2,0:T(1,128)S(1)}, s32[1,256,1]{1,2,0:T(1,128)}, u32[]{:S(2)}) copy-start(s32[1,256,1]{1,2,0:T(1,128)} %param.16) | copy-start | bytes 3076
  99.3 13.2 %copy-start.9 = (bf16[256,768]{0,1:T(8,128)(2,1)}, bf16[256,768]{0,1:T(8,128)(2,1)S(1)}, u32[]{:S(2)}) copy-start(bf16[256,768]{0,1:T(8,128)(2,1)S(1)} %copy.49) | copy-start | bytes 1179652
  101.6 27.7 %copy-start.37 = (s32[256]{0:T(256)}, s32[256]{0:T(256)S(1)}, u32[]{:S(2)}) copy-start(s32[256]{0:T(256)S(1)} %compare_select_fusion) | copy-start | bytes 3076
  115.0 8.4 %copy-start.2 = (f32[12,256,1024]{2,1,0:T(8,128)S(1)}, f32[12,256,1024]{2,1,0:T(8,128)}, u32[]{:S(2)}) copy-start(f32[12,256,1024]{2,1,0:T(8,128)} %get-tuple-element.33) | copy-start | bytes 37748740
  115.0 8.4 %copy-start.27 = (f32[12,256]{1,0:T(8,128)S(1)}, f32[12,256]{1,0:T(8,128)}, u32[]{:S(2)}) copy-start(f32[12,256]{1,0:T(8,128)} %get-tuple-element.32) | copy-start | bytes 36868
  130.6 13.7 %all-to-all-start = ((bf16[8,40,768]{2,1,0:T(8,128)(2,1)}), bf16[8,40,768]{2,1,0:T(8,128)(2,1)}, u32[]{:S(2)}, u32[]{:S(2)}) async-start(bf16[8,40,768]{2,1,0:T(8,128)(2,1)} %bitcast.214), calls=%async_computation | async-start | bytes 983040 | tf_op jit(solution)/shard_map/all_to_all | solution.py:144
  144.3 49.0 %all-to-all-start.2 = ((bf16[8,40,768]{2,1,0:T(8,128)(2,1)}), bf16[8,40,768]{2,1,0:T(8,128)(2,1)}, u32[]{:S(2)}, u32[]{:S(2)}) async-start(bf16[8,40,768]{2,1,0:T(8,128)(2,1)} %bitcast.213), calls=%async_computation.2 | async-start | bytes 983040 | tf_op jit(solution)/shard_map/all_to_all | solution.py:173
  287.8 17.7 %all-to-all-start.3 = ((bf16[8,2,15360]{2,1,0:T(2,128)(2,1)}), bf16[8,2,15360]{2,1,0:T(2,128)(2,1)}, u32[]{:S(2)}, u32[]{:S(2)}) async-start(bf16[8,2,15360]{2,1,0:T(2,128)(2,1)} %reshape.360), calls=%async_computation.3 | async-start | bytes 983040 | tf_op jit(solution)/shard_map/all_to_all | solution.py:190
  305.5 12.7 %all-to-all-start.1 = ((bf16[8,2,15360]{2,1,0:T(2,128)(2,1)}), bf16[8,2,15360]{2,1,0:T(2,128)(2,1)}, u32[]{:S(2)}, u32[]{:S(2)}) async-start(bf16[8,2,15360]{2,1,0:T(2,128)(2,1)} %reshape.358), calls=%async_computation.1 | async-start | bytes 983040 | tf_op jit(solution)/shard_map/all_to_all | solution.py:156
  309.7 109.2 %reduce-scatter.5.cloned.1.call-start = ((), (), s32[]{:S(2)}) async-start(), calls=%async_computation.10 | async-start | bytes 1966080 | tf_op jit(solution)/shard_map/reduce_scatter | solution.py:248
  334.1 12.5 %copy-start.21 = (bf16[1024,768]{0,1:T(8,128)(2,1)S(1)}, bf16[1024,768]{0,1:T(8,128)(2,1)}, u32[]{:S(2)}) copy-start(bf16[1024,768]{0,1:T(8,128)(2,1)} %copy.48) | copy-start | bytes 4718596
  334.1 12.5 %copy-start.24 = (bf16[256,768]{0,1:T(8,128)(2,1)S(1)}, bf16[256,768]{0,1:T(8,128)(2,1)}, u32[]{:S(2)}) copy-start(bf16[256,768]{0,1:T(8,128)(2,1)} %copy.53) | copy-start | bytes 1179652
  334.1 12.5 %copy-start.28 = (f32[12,256]{1,0:T(8,128)S(1)}, f32[12,256]{1,0:T(8,128)}, u32[]{:S(2)}) copy-start(f32[12,256]{1,0:T(8,128)} %get-tuple-element.32) | copy-start | bytes 36868
  334.1 12.5 %copy-start.41 = (f32[12,256]{1,0:T(8,128)S(1)}, f32[12,256]{1,0:T(8,128)}, u32[]{:S(2)}) copy-start(f32[12,256]{1,0:T(8,128)} %copy-done.40) | copy-start | bytes 36868
  356.8 70.0 %reduce-scatter.7.cloned.1.call-start = ((), (), s32[]{:S(2)}) async-start(), calls=%async_computation.11 | async-start | bytes 1966080 | tf_op jit(solution)/shard_map/reduce_scatter | solution.py:251
  364.9 168.5 %reduce-scatter.9.cloned.1.call-start = ((), (), s32[]{:S(2)}) async-start(), calls=%async_computation.12 | async-start | bytes 5898240 | tf_op jit(solution)/shard_map/reduce_scatter | solution.py:182
  371.6 230.6 %reduce-scatter.11.cloned.1.call-start = ((), (), s32[]{:S(2)}) async-start(), calls=%async_computation.13 | async-start | bytes 5898240 | tf_op jit(solution)/shard_map/reduce_scatter | solution.py:185
  378.0 423.4 %all-reduce.6.cloned.1.call-start = ((), (), s32[]{:S(2)}) async-start(), calls=%async_computation.16 | async-start | bytes 18874368 | tf_op jit(solution)/shard_map/psum | solution.py:273
  473.7 8.3 %copy-start.30 = (s32[1,256,1]{1,2,0:T(1,128)S(1)}, s32[1,256,1]{1,2,0:T(1,128)}, u32[]{:S(2)}) copy-start(s32[1,256,1]{1,2,0:T(1,128)} %param.16) | copy-start | bytes 3076
  473.7 8.3 %copy-start.34 = (f32[256]{0:T(256)S(1)}, f32[256]{0:T(256)}, u32[]{:S(2)}) copy-start(f32[256]{0:T(256)} %copy-done.33) | copy-start | bytes 3076
  473.7 8.3 %copy-start.36 = (f32[256]{0:T(256)S(1)}, f32[256]{0:T(256)}, u32[]{:S(2)}) copy-start(f32[256]{0:T(256)} %copy-done.35) | copy-start | bytes 3076
  473.8 9.1 %copy-start.14 = (bf16[12,64,256]{2,1,0:T(8,128)(2,1)S(1)}, bf16[12,64,256]{2,1,0:T(8,128)(2,1)}, u32[]{:S(2)}) copy-start(bf16[12,64,256]{2,1,0:T(8,128)(2,1)} %copy-done.13) | copy-start | bytes 1179652
  473.8 10.8 %copy-start.22 = (bf16[1,256,768]{1,2,0:T(8,128)(2,1)S(1)}, bf16[1,256,768]{1,2,0:T(8,128)(2,1)}, u32[]{:S(2)}) copy-start(bf16[1,256,768]{1,2,0:T(8,128)(2,1)} %reduce-scatter.5.cloned.1.call-done) | copy-start | bytes 1179652
  484.7 47.7 %copy-start.6 = (f32[256,768]{1,0:T(8,128)S(1)}, f32[256,768]{1,0:T(8,128)}, u32[]{:S(2)}) copy-start(f32[256,768]{1,0:T(8,128)} %copy-done.4) | copy-start | bytes 2359300
  484.7 47.7 %copy-start.47 = (f32[256]{0:T(256)S(1)}, f32[256]{0:T(256)}, u32[]{:S(2)}) copy-start(f32[256]{0:T(256)} %get-tuple-element.28) | copy-start | bytes 3076
  (34 other events, 144.9 us)
Sparse Core Ops, SparseCore 0:
  11.9 39.7 all-gather.12
  53.9 35.9 all-gather.10
  91.5 88.2 all-gather.6
  181.2 87.8 all-gather.8
  356.9 32.8 reduce-scatter.4
  392.5 34.2 reduce-scatter.6
  429.1 84.8 reduce-scatter.8
  516.4 85.7 reduce-scatter.10
  608.9 192.4 all-reduce.5
where the time goes:
time: 825 us; the launch traced here: 816 us
  waiting for transfers between devices  381 us (46%)
  local copies, waits for them, and re-layouts  181 us (22%)
  matrix products  126 us (15%)
  other arithmetic  51.3 us (6%)
  blocking collectives  44.1 us (5%)
  starting transfers between devices  18.1 us (2%)
  between operations  14.7 us (2%)
    psum x1, waiting for transfers between devices, shards(): lax.psum((grad_gain_attn, grad_query_w, grad_key_w, grad_value_w, grad_ou...  196 us
    all_gather x1, waiting for transfers between devices, shards(): lax.all_gather(w_out, 'ctx', axis=1, tiled=True)  75.7 us
    reduce_scatter x1, waiting for transfers between devices, shards(): lax.psum_scatter(full_second[None].astype(jnp.bfloat16), 'ctx', scatter_d...  65.9 us
    psum x1, blocking collectives, shards(): lax.psum((grad_gain_attn, grad_query_w, grad_key_w, grad_value_w, grad_ou...  44.1 us
    reshape x1, local copies, waits for them, and re-layouts, bias_block(): return skewed.reshape(heads, query_count, width - 1)[:, :, :key_count]  32.1 us
    all_gather x1, waiting for transfers between devices, shards(): lax.all_gather(w_in, 'ctx', axis=2, tiled=True)  31.3 us
    reshape x1, local copies, waits for them, and re-layouts, bias_grad_block(): return jnp.sum(flat.reshape(heads, query_count, width), axis=1)  31.2 us
    dot_general x9, matrix products, contract_rows(): lax.dot_general(left, right, (((0,), (0,)), ((), ())), preferred_element_...  27 us
  transfers between devices with their start and end apart: 13, of which 7 were waited for; matrix products, arithmetic and copies ran while one was open for 35% of the time, Pallas kernels for 0%

commit v1 on v0

--- a/solution.py
+++ b/solution.py
@@ -131,7 +131,9 @@
     )
     route_float = route_hot.astype(single)
     gate = jnp.sum(probs * route_float, axis=-1)
-    slot_index = jnp.sum((jnp.cumsum(route_hot, axis=0) - route_hot) * route_hot, axis=1)
+    earlier = jnp.tril(jnp.ones((tok_count, tok_count), bfloat), -1)
+    counts = jnp.dot(earlier, route_hot.astype(bfloat), preferred_element_type=single)
+    slot_index = jnp.sum(counts * route_float, axis=1).astype(jnp.int32)
     target = jnp.where(slot_index < capacity, route_flat * capacity + slot_index, -1)
     dispatch_mat = (
         target[:, None] == jnp.arange(experts * capacity, dtype=jnp.int32)[None, :]

time: 825 us -> 825 us (level)
  no operation moved by 1% of the time
where the time goes in v1:
time: 825 us; the launch traced here: 816 us
  waiting for transfers between devices  383 us (46%)
  local copies, waits for them, and re-layouts  181 us (22%)
  matrix products  126 us (15%)
  other arithmetic  49.1 us (6%)
  blocking collectives  44.2 us (5%)
  starting transfers between devices  18 us (2%)
  between operations  14.7 us (2%)
    psum x1, waiting for transfers between devices, shards(): lax.psum((grad_gain_attn, grad_query_w, grad_key_w, grad_value_w, grad_ou...  196 us
    all_gather x1, waiting for transfers between devices, shards(): lax.all_gather(w_out, 'ctx', axis=1, tiled=True)  75.7 us
    reduce_scatter x1, waiting for transfers between devices, shards(): lax.psum_scatter(full_second[None].astype(jnp.bfloat16), 'ctx', scatter_d...  65.9 us
    psum x1, blocking collectives, shards(): lax.psum((grad_gain_attn, grad_query_w, grad_key_w, grad_value_w, grad_ou...  44.2 us
    all_gather x1, waiting for transfers between devices, shards(): lax.all_gather(w_in, 'ctx', axis=2, tiled=True)  33.4 us
    reshape x1, local copies, waits for them, and re-layouts, bias_block(): return skewed.reshape(heads, query_count, width - 1)[:, :, :key_count]  32.1 us
    reshape x1, local copies, waits for them, and re-layouts, bias_grad_block(): return jnp.sum(flat.reshape(heads, query_count, width), axis=1)  31.2 us
    dot_general x9, matrix products, contract_rows(): lax.dot_general(left, right, (((0,), (0,)), ((), ())), preferred_element_...  27 us
  transfers between devices with their start and end apart: 13, of which 7 were waited for; matrix products, arithmetic and copies ran while one was open for 35% of the time, Pallas kernels for 0%

profile of v1, /device:TPU:0, one launch (start us, length us, event | category | flops | bytes accessed | tf_op | source)
XLA Modules:
  0.0 815.8 jit_solution(6900315371581373434)
XLA Ops:
  16.5 6.8 broadcast_in_dim.14
  23.3 25.2 %reshape.321 = f32[12,327424]{1,0:T(8,128)} reshape(f32[12,256,1279]{2,1,0:T(8,128)} %broadcast_in_dim.14) | data formatting | bytes 31432704 | tf_op jit(solution)/shard_map/reshape | solution.py:47
  48.5 17.8 %slice.10 = f32[12,327168]{1,0:T(8,128)} slice(f32[12,327424]{1,0:T(8,128)} %reshape.321), slice={[0:12], [255:327423]} | slice | bytes 31408128 | tf_op jit(solution)/shard_map/slice | solution.py:50
  66.4 32.1 %reshape.322 = f32[12,256,1278]{2,1,0:T(8,128)} reshape(f32[12,327168]{1,0:T(8,128)} %slice.10) | data formatting | bytes 31408128 | tf_op jit(solution)/shard_map/reshape | solution.py:51
  101.3 9.0 %fusion.119 = (f32[12,256]{1,0:T(8,128)}, f32[12,256,1024]{2,1,0:T(8,128)}) fusion(f32[12,256,1278]{2,1,0:T(8,128)} %reshape.322, bf16[256,12,64]{0,2,1:T(8,128)(2,1)S(1)} %bitcast.200, bf16[1024,12,64]{0,2,1:T(8,128)(2,1)S(1)} %bitcast.197), kind=kOutput, calls=%fused_computation.150 | convolution fusion | flops 408941568 | bytes 27144192 | tf_op jit(solution)/shard_map/sqhd,skhd->shqk/dot_general | solution.py:108
  113.0 7.7 fusion.1
  121.4 4.2 fusion.34
  128.5 5.0 all-to-all-start
  146.3 33.4 %all-gather.7.cloned.1.call-done = bf16[1,768,3072]{2,1,0:T(8,128)(2,1)} async-done(((bf16[1,768,768]{2,1,0:T(8,128)(2,1)}), bf16[1,768,3072]{2,1,0:T(8,128)(2,1)}) %all-gather.7.cloned.1.call-update) | async-done | bytes 4718608 | tf_op jit(solution)/shard_map/all_gather | solution.py:149
  179.7 13.6 %multiply_convert_fusion.1 = (bf16[320,3072]{1,0:T(8,128)(2,1)}, f32[320,3072]{1,0:T(8,128)}, f32[320,3072]{1,0:T(8,128)}) fusion(bf16[320,768]{1,0:T(8,128)(2,1)} %bitcast.10, bf16[1,768,3072]{2,1,0:T(8,128)(2,1)} %all-gather.7.cloned.1.call-done), kind=kOutput, calls=%fused_computation.21 | convolution fusion | flops 1573847040 | bytes 15040512 | tf_op jit(solution)/shard_map/dot_general | solution.py:154
  193.3 75.7 %all-gather.9.cloned.1.call-done = bf16[1,3072,768]{2,1,0:T(8,128)(2,1)} async-done(((bf16[1,768,768]{2,1,0:T(8,128)(2,1)}), bf16[1,3072,768]{2,1,0:T(8,128)(2,1)}) %all-gather.9.cloned.1.call-update) | async-done | bytes 4718608 | tf_op jit(solution)/shard_map/all_gather | solution.py:150
  269.0 7.4 add_convert_fusion
  280.4 5.3 reduce.5
  287.7 4.1 all-to-all-start.3
  291.9 4.6 fusion.37
  298.2 5.3 reduce.6
  305.5 4.1 all-to-all-start.1
  334.0 12.5 %fusion.43 = f32[256,12]{0,1:T(8,128)S(1)} fusion(f32[1,256,12,64]{1,3,2,0:T(8,128)} %bitcast.216, bf16[1024,12,64]{0,2,1:T(8,128)(2,1)} %bitcast.213, f32[12,256,1024]{2,1,0:T(8,128)} %get-tuple-element.33, f32[12,256]{1,0:T(8,128)} %copy-done.40, f32[12,256]{1,0:T(8,128)} %get-tuple-element.32), kind=kOutput, calls=%fused_computation.59 | convolution fusion | flops 2422600704 | bytes 14979072 | tf_op jit(solution)/shard_map/shqk,skhd->sqhd/dot_general | solution.py:119
  346.6 7.0 multiply_convert_fusion
  356.8 8.0 fusion.24
  365.0 6.5 fusion.10
  371.6 6.4 fusion.11
  378.0 6.8 pad.10
  384.8 24.4 %reshape.328 = bf16[12,327168]{1,0:T(8,128)(2,1)} reshape(bf16[12,256,1278]{2,1,0:T(8,128)(2,1)} %pad.10) | data formatting | bytes 15704064 | tf_op jit(solution)/shard_map/reshape | solution.py:58
  409.2 4.9 convolution_convert_fusion.5
  421.8 5.0 reduce-scatter.7.cloned.1.call-done
  429.8 12.5 %pad_convert_fusion = f32[12,327424]{1,0:T(8,128)} fusion(bf16[12,327168]{1,0:T(8,128)(2,1)} %reshape.328), kind=kLoop, calls=%fused_computation.5 | loop fusion | flops 3929088 | bytes 23568384 | tf_op jit(solution)/shard_map/reshape | solution.py:60
  442.3 31.2 %reshape.335 = f32[12,256,1279]{2,1,0:T(8,128)} reshape(f32[12,327424]{1,0:T(8,128)} %pad_convert_fusion) | data formatting | bytes 31432704 | tf_op jit(solution)/shard_map/reshape | solution.py:60
  473.7 6.4 reduce_sum.135
  488.1 44.2 %all-reduce.2 = (f32[768]{0:T(1024)}, f32[32,12]{0,1:T(8,128)}, f32[768]{0:T(1024)}, f32[768,8]{0,1:T(8,128)}) all-reduce(f32[768]{0:T(1024)S(1)} %get-tuple-element.14, f32[32,12]{0,1:T(8,128)S(1)} %copy-done.46, f32[768]{0:T(1024)S(1)} %copy-done.42, ...), channel_id=1, replica_groups=mesh['dp'=4,'ctx'=4,'expert'=2] {'dp','ctx','expert'}, use_global_device_ids=true, to_apply=%region_15.16 | all-reduce | flops 8064 | bytes 64512 | tf_op jit(solution)/shard_map/psum | solution.py:275
  536.2 65.9 %reduce-scatter.11.cloned.1.call-done = bf16[1,768,768]{2,1,0:T(8,128)(2,1)} async-done(((bf16[1,3072,768]{2,1,0:T(8,128)(2,1)}), bf16[1,768,768]{2,1,0:T(8,128)(2,1)}) %reduce-scatter.11.cloned.1.call-update) | async-done | bytes 1179664 | tf_op jit(solution)/shard_map/reduce_scatter | solution.py:187
  604.9 196.5 %all-reduce.6.cloned.1.call-done = (f32[768,768]{1,0:T(8,128)}, f32[768,768]{1,0:T(8,128)}, f32[768,768]{1,0:T(8,128)}, f32[768,768]{1,0:T(8,128)}) async-done(((f32[768,768]{1,0:T(8,128)}, f32[768,768]{1,0:T(8,128)}, f32[768,768]{1,0:T(8,128)}, f32[768,768]{1,0:T(8,128)}), (f32[768,768]{1,0:T(8,128)}, f32[768,768]{1,0:T(8,128)}, f32[768,768]{1,0:T(8,128)}, ...) | async-done | bytes 9437200 | tf_op jit(solution)/shard_map/psum | solution.py:275
  (190 shorter events, 101.2 us)
Async XLA Ops:
  7.2 92.3 %all-gather.13.cloned.1.call-start = ((), (), s32[]{:S(2)}) async-start(), calls=%async_computation.15 | async-start | bytes 1966080 | tf_op jit(solution)/shard_map/all_gather | solution.py:102
  11.8 98.6 %all-gather.11.cloned.1.call-start = ((), (), s32[]{:S(2)}) async-start(), calls=%async_computation.14 | async-start | bytes 1966080 | tf_op jit(solution)/shard_map/all_gather | solution.py:103
  14.1 165.6 %all-gather.7.cloned.1.call-start = ((), (), s32[]{:S(2)}) async-start(), calls=%async_computation.8 | async-start | bytes 5898240 | tf_op jit(solution)/shard_map/all_gather | solution.py:149
  14.9 254.1 %all-gather.9.cloned.1.call-start = ((), (), s32[]{:S(2)}) async-start(), calls=%async_computation.9 | async-start | bytes 5898240 | tf_op jit(solution)/shard_map/all_gather | solution.py:150
  66.4 32.1 %copy-start.3 = (bf16[1,256,768]{2,1,0:T(8,128)(2,1)S(1)}, bf16[1,256,768]{2,1,0:T(8,128)(2,1)}, u32[]{:S(2)}) copy-start(bf16[1,256,768]{2,1,0:T(8,128)(2,1)} %param.14) | copy-start | bytes 1179652
  66.4 32.1 %copy-start.23 = (bf16[768,768]{1,0:T(8,128)(2,1)S(1)}, bf16[768,768]{1,0:T(8,128)(2,1)}, u32[]{:S(2)}) copy-start(bf16[768,768]{1,0:T(8,128)(2,1)} %param.19) | copy-start | bytes 3538948
  66.4 32.1 %copy-start.25 = (f32[768]{0:T(1024)S(1)}, f32[768]{0:T(1024)}, u32[]{:S(2)}) copy-start(f32[768]{0:T(1024)} %param.18) | copy-start | bytes 9220
  66.4 32.8 %copy-start.36 = (s32[1,256,1]{1,2,0:T(1,128)S(1)}, s32[1,256,1]{1,2,0:T(1,128)}, u32[]{:S(2)}) copy-start(s32[1,256,1]{1,2,0:T(1,128)} %param.16) | copy-start | bytes 3076
  99.2 11.2 %copy-start.9 = (bf16[256,768]{0,1:T(8,128)(2,1)}, bf16[256,768]{0,1:T(8,128)(2,1)S(1)}, u32[]{:S(2)}) copy-start(bf16[256,768]{0,1:T(8,128)(2,1)S(1)} %copy.49) | copy-start | bytes 1179652
  99.5 27.8 %copy-start.35 = (s32[256]{0:T(256)}, s32[256]{0:T(256)S(1)}, u32[]{:S(2)}) copy-start(s32[256]{0:T(256)S(1)} %compare_select_fusion) | copy-start | bytes 3076
  113.0 8.4 %copy-start.2 = (f32[12,256,1024]{2,1,0:T(8,128)S(1)}, f32[12,256,1024]{2,1,0:T(8,128)}, u32[]{:S(2)}) copy-start(f32[12,256,1024]{2,1,0:T(8,128)} %get-tuple-element.33) | copy-start | bytes 37748740
  113.0 8.4 %copy-start.27 = (f32[12,256]{1,0:T(8,128)S(1)}, f32[12,256]{1,0:T(8,128)}, u32[]{:S(2)}) copy-start(f32[12,256]{1,0:T(8,128)} %get-tuple-element.32) | copy-start | bytes 36868
  128.5 13.6 %all-to-all-start = ((bf16[8,40,768]{2,1,0:T(8,128)(2,1)}), bf16[8,40,768]{2,1,0:T(8,128)(2,1)}, u32[]{:S(2)}, u32[]{:S(2)}) async-start(bf16[8,40,768]{2,1,0:T(8,128)(2,1)} %bitcast.209), calls=%async_computation | async-start | bytes 983040 | tf_op jit(solution)/shard_map/all_to_all | solution.py:146
  142.1 51.2 %all-to-all-start.2 = ((bf16[8,40,768]{2,1,0:T(8,128)(2,1)}), bf16[8,40,768]{2,1,0:T(8,128)(2,1)}, u32[]{:S(2)}, u32[]{:S(2)}) async-start(bf16[8,40,768]{2,1,0:T(8,128)(2,1)} %bitcast.208), calls=%async_computation.2 | async-start | bytes 983040 | tf_op jit(solution)/shard_map/all_to_all | solution.py:175
  287.7 17.7 %all-to-all-start.3 = ((bf16[8,2,15360]{2,1,0:T(2,128)(2,1)}), bf16[8,2,15360]{2,1,0:T(2,128)(2,1)}, u32[]{:S(2)}, u32[]{:S(2)}) async-start(bf16[8,2,15360]{2,1,0:T(2,128)(2,1)} %reshape.343), calls=%async_computation.3 | async-start | bytes 983040 | tf_op jit(solution)/shard_map/all_to_all | solution.py:192
  305.5 12.7 %all-to-all-start.1 = ((bf16[8,2,15360]{2,1,0:T(2,128)(2,1)}), bf16[8,2,15360]{2,1,0:T(2,128)(2,1)}, u32[]{:S(2)}, u32[]{:S(2)}) async-start(bf16[8,2,15360]{2,1,0:T(2,128)(2,1)} %reshape.341), calls=%async_computation.1 | async-start | bytes 983040 | tf_op jit(solution)/shard_map/all_to_all | solution.py:158
  309.6 109.2 %reduce-scatter.5.cloned.1.call-start = ((), (), s32[]{:S(2)}) async-start(), calls=%async_computation.10 | async-start | bytes 1966080 | tf_op jit(solution)/shard_map/reduce_scatter | solution.py:250
  334.0 12.5 %copy-start.21 = (bf16[1024,768]{0,1:T(8,128)(2,1)S(1)}, bf16[1024,768]{0,1:T(8,128)(2,1)}, u32[]{:S(2)}) copy-start(bf16[1024,768]{0,1:T(8,128)(2,1)} %copy.48) | copy-start | bytes 4718596
  334.0 12.5 %copy-start.24 = (bf16[256,768]{0,1:T(8,128)(2,1)S(1)}, bf16[256,768]{0,1:T(8,128)(2,1)}, u32[]{:S(2)}) copy-start(bf16[256,768]{0,1:T(8,128)(2,1)} %copy.53) | copy-start | bytes 1179652
  334.0 12.5 %copy-start.28 = (f32[12,256]{1,0:T(8,128)S(1)}, f32[12,256]{1,0:T(8,128)}, u32[]{:S(2)}) copy-start(f32[12,256]{1,0:T(8,128)} %get-tuple-element.32) | copy-start | bytes 36868
  334.0 12.5 %copy-start.41 = (f32[12,256]{1,0:T(8,128)S(1)}, f32[12,256]{1,0:T(8,128)}, u32[]{:S(2)}) copy-start(f32[12,256]{1,0:T(8,128)} %copy-done.40) | copy-start | bytes 36868
  356.8 70.0 %reduce-scatter.7.cloned.1.call-start = ((), (), s32[]{:S(2)}) async-start(), calls=%async_computation.11 | async-start | bytes 1966080 | tf_op jit(solution)/shard_map/reduce_scatter | solution.py:253
  364.8 168.5 %reduce-scatter.9.cloned.1.call-start = ((), (), s32[]{:S(2)}) async-start(), calls=%async_computation.12 | async-start | bytes 5898240 | tf_op jit(solution)/shard_map/reduce_scatter | solution.py:184
  371.5 230.6 %reduce-scatter.11.cloned.1.call-start = ((), (), s32[]{:S(2)}) async-start(), calls=%async_computation.13 | async-start | bytes 5898240 | tf_op jit(solution)/shard_map/reduce_scatter | solution.py:187
  378.0 423.5 %all-reduce.6.cloned.1.call-start = ((), (), s32[]{:S(2)}) async-start(), calls=%async_computation.16 | async-start | bytes 18874368 | tf_op jit(solution)/shard_map/psum | solution.py:275
  473.6 8.3 %copy-start.32 = (f32[256]{0:T(256)S(1)}, f32[256]{0:T(256)}, u32[]{:S(2)}) copy-start(f32[256]{0:T(256)} %copy-done.31) | copy-start | bytes 3076
  473.6 8.3 %copy-start.34 = (f32[256]{0:T(256)S(1)}, f32[256]{0:T(256)}, u32[]{:S(2)}) copy-start(f32[256]{0:T(256)} %copy-done.33) | copy-start | bytes 3076
  473.6 8.3 %copy-start.37 = (s32[1,256,1]{1,2,0:T(1,128)S(1)}, s32[1,256,1]{1,2,0:T(1,128)}, u32[]{:S(2)}) copy-start(s32[1,256,1]{1,2,0:T(1,128)} %param.16) | copy-start | bytes 3076
  473.6 9.1 %copy-start.14 = (bf16[12,64,256]{2,1,0:T(8,128)(2,1)S(1)}, bf16[12,64,256]{2,1,0:T(8,128)(2,1)}, u32[]{:S(2)}) copy-start(bf16[12,64,256]{2,1,0:T(8,128)(2,1)} %copy-done.13) | copy-start | bytes 1179652
  473.6 10.8 %copy-start.22 = (bf16[1,256,768]{1,2,0:T(8,128)(2,1)S(1)}, bf16[1,256,768]{1,2,0:T(8,128)(2,1)}, u32[]{:S(2)}) copy-start(bf16[1,256,768]{1,2,0:T(8,128)(2,1)} %reduce-scatter.5.cloned.1.call-done) | copy-start | bytes 1179652
  484.5 47.8 %copy-start.6 = (f32[256,768]{1,0:T(8,128)S(1)}, f32[256,768]{1,0:T(8,128)}, u32[]{:S(2)}) copy-start(f32[256,768]{1,0:T(8,128)} %copy-done.4) | copy-start | bytes 2359300
  484.5 47.8 %copy-start.47 = (f32[256]{0:T(256)S(1)}, f32[256]{0:T(256)}, u32[]{:S(2)}) copy-start(f32[256]{0:T(256)} %get-tuple-element.28) | copy-start | bytes 3076
  (34 other events, 144.7 us)
Sparse Core Ops, SparseCore 0:
  11.9 39.7 all-gather.12
  53.8 35.9 all-gather.10
  91.4 88.2 all-gather.6
  181.1 87.8 all-gather.8
  356.9 32.8 reduce-scatter.4
  392.5 34.2 reduce-scatter.6
  429.1 84.9 reduce-scatter.8
  516.3 85.7 reduce-scatter.10
  608.9 192.4 all-reduce.5

commit v2 on v0

v2 whole, which is shorter than its diff:
```python
import functools

import jax
import jax.numpy as jnp
from jax import lax
from jax.experimental import pallas as pl
from jax.experimental.pallas import tpu as pltpu
from jax.sharding import PartitionSpec as P

H = 12
HD = 64
NB = 32
PLANE = ("dp", "expert")

epsilon = 1e-06
exact_prec = lax.Precision.HIGHEST
bfloat = jnp.bfloat16
single = jnp.float32
VMEM_LIMIT = 56 * 1024 * 1024


def norm_scale(row_data):
    return lax.rsqrt(jnp.mean(row_data * row_data, axis=-1, keepdims=True) + epsilon)


def norm_back(grad_in, row_data, scale, gain):
    weighted = grad_in * gain
    inner = jnp.mean(weighted * row_data, axis=-1, keepdims=True)
    return scale * weighted - row_data * (scale * scale * scale) * inner


def dot_nn(left, right):
    return lax.dot_general(
        left, right, (((1,), (0,)), ((), ())), preferred_element_type=single
    )


def dot_nt(left, right):
    return lax.dot_general(
        left, right, (((1,), (1,)), ((), ())), preferred_element_type=single
    )


def dot_tn(left, right):
    return lax.dot_general(
        left, right, (((0,), (0,)), ((), ())), preferred_element_type=single
    )


def pack_rows(rows):
    half = rows.shape[0] // 2
    return jnp.concatenate([rows[:half], rows[half:]], axis=1)


def unpack_rows(packed):
    width = packed.shape[1] // 2
    return jnp.concatenate([packed[:, :width], packed[:, width:]], axis=0)


def bias_strip(rel_row, rows, width):
    spread = jnp.broadcast_to(rel_row, (rows, width))
    return pltpu.roll(spread, width - (rows - 1), 1, stride=1, stride_axis=0)


def fold_strip(strip):
    rows = strip.shape[0]
    while rows > 1:
        rows //= 2
        strip = strip[rows:] + pltpu.roll(strip[:rows], rows, 1)
    return strip


def attend_kernel(n, heads, place_ref, *refs):
    blocks = refs[:n]
    gain_ref, w_ref, rel_ref, normed_ref, qkv_ref, lse_ref, out_ref, strip_ref = refs[n:]
    place = place_ref[0]
    block_len = blocks[0].shape[0]
    full_len = n * block_len
    width = heads * HD
    for r in range(n):
        start = pl.multiple_of(lax.rem(place - r + n, n) * block_len, block_len)
        row_data = blocks[r][...].astype(single)
        normed = (row_data * norm_scale(row_data) * gain_ref[...]).astype(bfloat)
        normed_ref[pl.ds(start, block_len), :] = normed
        qkv_ref[pl.ds(start, block_len), :] = dot_nn(normed, w_ref[...]).astype(bfloat)
    for h in range(heads):
        strip_ref[h] = bias_strip(rel_ref[h : h + 1, :], block_len, 2 * full_len)
    lse_ref[...] = jnp.zeros_like(lse_ref)

    def tile(t, carry):
        rows = pl.ds(pl.multiple_of(t * block_len, block_len), block_len)
        skew = pl.ds(pl.multiple_of((n - 1 - t) * block_len, block_len), full_len)
        made = []
        for h in range(heads):
            query = qkv_ref[rows, h * HD : (h + 1) * HD]
            key = qkv_ref[:, width + h * HD : width + (h + 1) * HD]
            value = qkv_ref[:, 2 * width + h * HD : 2 * width + (h + 1) * HD]
            scores = dot_nt(query, key) + strip_ref[h, :, skew]
            top = jnp.max(scores, axis=1, keepdims=True)
            expd = jnp.exp(scores - top)
            total = jnp.sum(expd, axis=1, keepdims=True)
            made.append(dot_nn(expd.astype(bfloat), value) / total)
            lse_ref[rows, h : h + 1] = top + jnp.log(total)
        joined = jnp.concatenate(made, axis=1).astype(bfloat)
        out_ref[lax.rem(t - place + n, n)] = pack_rows(joined)
        return carry

    lax.fori_loop(0, n, tile, 0)


def attend(place, blocks, gain, w_local, rel, heads):
    n = len(blocks)
    block_len, model_width = blocks[0].shape
    full_len = n * block_len
    width = heads * HD
    vmem = pl.BlockSpec(memory_space=pltpu.VMEM)
    return pl.pallas_call(
        functools.partial(attend_kernel, n, heads),
        out_shape=(
            jax.ShapeDtypeStruct((full_len, model_width), bfloat),
            jax.ShapeDtypeStruct((full_len, 3 * width), bfloat),
            jax.ShapeDtypeStruct((full_len, 128), single),
            jax.ShapeDtypeStruct((n, block_len // 2, 2 * width), bfloat),
        ),
        in_specs=[pl.BlockSpec(memory_space=pltpu.SMEM)] + [vmem] * (n + 3),
        out_specs=(vmem,) * 4,
        scratch_shapes=[pltpu.VMEM((heads, block_len, 2 * full_len), single)],
        compiler_params=pltpu.CompilerParams(vmem_limit_bytes=VMEM_LIMIT),
        cost_estimate=pl.CostEstimate(
            flops=2 * full_len * width * (3 * model_width + 2 * full_len),
            bytes_accessed=8 * full_len * model_width,
            transcendentals=heads * full_len * full_len,
        ),
        name="attend",
    )(place, *blocks, gain, w_local, rel)


def attend_back_kernel(n, heads, place_ref, *refs):
    blocks = refs[:n]
    (qkv_ref, lse_ref, rel_ref, w_ref, normed_ref, gain_ref,
     dqkv_ref, part_ref, gain_out_ref, rel_out_ref,
     da_ref, strip_ref, sums_ref, key_acc, value_acc) = refs[n:]
    place = place_ref[0]
    block_len = blocks[0].shape[0] * 2
    full_len = n * block_len
    width = heads * HD
    for r in range(n):
        start = pl.multiple_of(lax.rem(place + r, n) * block_len, block_len)
        da_ref[pl.ds(start, block_len), :] = unpack_rows(blocks[r][...])
    for h in range(heads):
        strip_ref[...] = bias_strip(rel_ref[h : h + 1, :], block_len, 2 * full_len)
        sums_ref[...] = jnp.zeros_like(sums_ref)
        key_acc[...] = jnp.zeros_like(key_acc)
        value_acc[...] = jnp.zeros_like(value_acc)

        def tile(t, carry, h=h):
            rows = pl.ds(pl.multiple_of(t * block_len, block_len), block_len)
            skew = pl.ds(pl.multiple_of((n - 1 - t) * block_len, block_len), full_len)
            query = qkv_ref[rows, h * HD : (h + 1) * HD]
            key = qkv_ref[:, width + h * HD : width + (h + 1) * HD]
            value = qkv_ref[:, 2 * width + h * HD : 2 * width + (h + 1) * HD]
            grad_attn = da_ref[rows, h * HD : (h + 1) * HD]
            scores = dot_nt(query, key) + strip_ref[:, skew]
            soft = jnp.exp(scores - lse_ref[rows, h : h + 1])
            value_acc[...] += dot_tn(grad_attn, soft.astype(bfloat))
            grad_soft = dot_nt(grad_attn, value)
            delta = jnp.sum(soft * grad_soft, axis=1, keepdims=True)
            grad_wide = soft * (grad_soft - delta)
            sums_ref[:, skew] += grad_wide
            grad_scores = grad_wide.astype(bfloat)
            dqkv_ref[rows, h * HD : (h + 1) * HD] = dot_nn(grad_scores, key).astype(bfloat)
            key_acc[...] += dot_tn(query, grad_scores)
            return carry

        lax.fori_loop(0, n, tile, 0)
        dqkv_ref[:, width + h * HD : width + (h + 1) * HD] = key_acc[...].T.astype(bfloat)
        dqkv_ref[:, 2 * width + h * HD : 2 * width + (h + 1) * HD] = (
            value_acc[...].T.astype(bfloat)
        )
        rel_out_ref[h : h + 1, :] = fold_strip(sums_ref[...])
    total = jnp.zeros((1, normed_ref.shape[1]), single)
    for r in range(n):
        start = pl.multiple_of(lax.rem(place + r, n) * block_len, block_len)
        rows = pl.ds(start, block_len)
        part = dot_nt(dqkv_ref[rows, :], w_ref[...])
        total += jnp.sum(part * normed_ref[rows, :].astype(single), axis=0, keepdims=True)
        part_ref[r] = part.astype(bfloat)
    gain_out_ref[...] = total / gain_ref[...]


def attend_back(place, blocks, qkv, lse, rel, w_local, normed, gain, heads):
    n = len(blocks)
    full_len, model_width = normed.shape
    block_len = full_len // n
    width = heads * HD
    vmem = pl.BlockSpec(memory_space=pltpu.VMEM)
    return pl.pallas_call(
        functools.partial(attend_back_kernel, n, heads),
        out_shape=(
            jax.ShapeDtypeStruct((full_len, 3 * width), bfloat),
            jax.ShapeDtypeStruct((n, block_len, model_width), bfloat),
            jax.ShapeDtypeStruct((1, model_width), single),
            jax.ShapeDtypeStruct((heads, 2 * full_len), single),
        ),
        in_specs=[pl.BlockSpec(memory_space=pltpu.SMEM)] + [vmem] * (n + 6),
        out_specs=(vmem,) * 4,
        scratch_shapes=[
            pltpu.VMEM((full_len, width), bfloat),
            pltpu.VMEM((block_len, 2 * full_len), single),
            pltpu.VMEM((block_len, 2 * full_len), single),
            pltpu.VMEM((HD, full_len), single),
            pltpu.VMEM((HD, full_len), single),
        ],
        compiler_params=pltpu.CompilerParams(vmem_limit_bytes=VMEM_LIMIT),
        cost_estimate=pl.CostEstimate(
            flops=2 * full_len * width * (3 * model_width + 5 * full_len),
            bytes_accessed=8 * full_len * model_width,
            transcendentals=heads * full_len * full_len,
        ),
        name="attend_back",
    )(place, *blocks, qkv, lse, rel, w_local, normed, gain)


def shift(block, by):
    n = lax.axis_size("ctx")
    return lax.ppermute(block, "ctx", [(i, (i + by) % n) for i in range(n)])


def swap_plane(block, mask):
    count = lax.axis_size(PLANE)
    return lax.ppermute(block, PLANE, [(i, i ^ mask) for i in range(count)])


def to_plane(blocks):
    return lax.all_to_all(blocks, PLANE, split_axis=0, concat_axis=0, tiled=True)


def sum_plane(piece):
    count = lax.axis_size(PLANE)
    rows, width = piece.shape
    parts = to_plane(piece.astype(bfloat).reshape(count, rows // count, width))
    return jnp.sum(parts.astype(single), axis=0).astype(bfloat)


def gather_all(piece):
    n = lax.axis_size("ctx")
    count = lax.axis_size(PLANE)
    stack = jnp.stack([piece] + [shift(piece, r) for r in range(1, n)])
    core = lax.axis_size("expert")
    held = {0: stack}
    for mask in range(1, count):
        if not mask & core:
            held[mask] = swap_plane(stack, mask)
    for mask in list(held):
        held[mask | core] = swap_plane(held[mask], core)
    return [held[mask] for mask in range(count)]


def place_late_kernel(count, n, width, spot_ref, *refs):
    spot, place = spot_ref[0], spot_ref[1]
    ins, outs, extra_ref = refs[:count], refs[count : count + 3], refs[count + 3]
    step = ins[0].shape[1]
    for mask in range(count):
        rows = pl.ds(pl.multiple_of((spot ^ mask) * step, step), step)
        for c in range(n):
            block = ins[mask][lax.rem(place - c + n, n)].astype(single)
            for i in range(3):
                outs[i][rows, c * width : (c + 1) * width] = block[:, i * width : (i + 1) * width]
            extra_ref[c, rows, :] = block[:, 3 * width :]


def place_output_kernel(count, n, spot_ref, *refs):
    spot, place = spot_ref[0], spot_ref[1]
    step = refs[0].shape[1]
    for mask in range(count):
        for c in range(n):
            start = (c * count + (spot ^ mask)) * step
            block = refs[mask][lax.rem(place - c + n, n)]
            refs[count][pl.ds(pl.multiple_of(start, step), step), :] = block.astype(single)


def placed(kernel, spots, held, shapes):
    vmem = pl.BlockSpec(memory_space=pltpu.VMEM)
    return pl.pallas_call(
        kernel,
        out_shape=[jax.ShapeDtypeStruct(s, single) for s in shapes],
        in_specs=[pl.BlockSpec(memory_space=pltpu.SMEM)] + [vmem] * len(held),
        out_specs=[vmem] * len(shapes),
        compiler_params=pltpu.CompilerParams(vmem_limit_bytes=VMEM_LIMIT),
        cost_estimate=pl.CostEstimate(flops=0, bytes_accessed=12_000_000, transcendentals=0),
        name="placed",
    )(spots, *held)


def gather_late(piece, width, model_width):
    n = lax.axis_size("ctx")
    count = lax.axis_size(PLANE)
    if piece.shape[0] % 8:
        whole = lax.all_gather(lax.all_gather(piece, "ctx"), PLANE).astype(single)
        whole = whole.transpose(1, 0, 2, 3).reshape(n, model_width, -1)
        own = [whole[:, :, i * width : (i + 1) * width] for i in range(3)]
        own = [o.transpose(1, 0, 2).reshape(model_width, n * width) for o in own]
        return own + [whole[:, :, 3 * width :]]
    spots = jnp.stack([lax.axis_index(PLANE), lax.axis_index("ctx")]).astype(jnp.int32)
    shapes = [(model_width, n * width)] * 3 + [(n, model_width, piece.shape[1] - 3 * width)]
    kernel = functools.partial(place_late_kernel, count, n, width)
    return placed(kernel, spots, gather_all(piece), shapes)


def gather_output(piece):
    n = lax.axis_size("ctx")
    count = lax.axis_size(PLANE)
    rows = n * count * piece.shape[0]
    if piece.shape[0] % 8:
        whole = lax.all_gather(lax.all_gather(piece, "ctx"), PLANE).astype(single)
        return whole.transpose(1, 0, 2, 3).reshape(rows, -1)
    spots = jnp.stack([lax.axis_index(PLANE), lax.axis_index("ctx")]).astype(jnp.int32)
    kernel = functools.partial(place_output_kernel, count, n)
    return placed(kernel, spots, gather_all(piece), [(rows, piece.shape[1])])[0]


def shards(
    tokens,
    cotangent,
    routes,
    buckets,
    gain_attn,
    w_query,
    w_key,
    w_value,
    w_output,
    bias_table,
    gain_ffn,
    w_router,
    w_in,
    w_out,
):
    seq_dev, block_len, model_width = tokens.shape
    n = lax.axis_size("ctx")
    experts = lax.axis_size(PLANE)
    heads = H // n
    width = heads * HD
    full_len = block_len * n
    tok_count = seq_dev * block_len
    capacity = max(2, (5 * tok_count + 4 * experts - 1) // (4 * experts))
    slots = experts * capacity
    place = lax.axis_index("ctx")
    spot = lax.axis_index(PLANE)
    place_in = place.astype(jnp.int32).reshape(1)

    block = tokens.reshape(tok_count, model_width)
    blocks = [block] + [shift(block, r) for r in range(1, n)]
    row_data = block.astype(single)

    own_heads = [
        lax.dynamic_slice_in_dim(w, place * width, width, 1) for w in (w_query, w_key, w_value)
    ]
    w_local = jnp.concatenate(own_heads, axis=1)
    turned = [
        lax.dynamic_slice_in_dim(w_output, (place - r) % n * width, width, 0) for r in range(n)
    ]
    w_turned = jnp.concatenate(turned, axis=0)
    bucket_hot = (buckets[:, None] == jnp.arange(NB, dtype=jnp.int32)[None, :]).astype(single)
    table_local = lax.dynamic_slice_in_dim(bias_table, place * heads, heads, 1)
    rel = lax.dot_general(
        table_local, bucket_hot, (((0,), (1,)), ((), ())), precision=exact_prec
    )
    rel = jnp.pad(rel, ((0, 0), (0, 1)))
    route_flat = routes.reshape(tok_count)
    route_hot = (
        route_flat[:, None] == jnp.arange(experts, dtype=jnp.int32)[None, :]
    ).astype(bfloat)
    earlier = jnp.tril(jnp.ones((tok_count, tok_count), bfloat), -1)
    counts = dot_nn(earlier, route_hot)
    slot_index = jnp.sum(counts * route_hot.astype(single), axis=1).astype(jnp.int32)
    target = jnp.where(slot_index < capacity, route_flat * capacity + slot_index, -1)
    dispatch_mat = (target[:, None] == jnp.arange(slots, dtype=jnp.int32)[None, :]).astype(bfloat)

    grad_block = cotangent.reshape(tok_count, model_width)
    grad_in = grad_block.astype(single)
    grad_sent = dot_tn(dispatch_mat, grad_block).astype(bfloat)
    grad_near = to_plane(grad_sent.reshape(experts, capacity, model_width))
    grad_near = grad_near.reshape(slots, model_width)

    normed_all, qkv, lse, attn_parts = attend(
        place_in, blocks, gain_attn.reshape(1, -1), w_local, rel, heads
    )
    tied = lax.optimization_barrier((attn_parts, grad_near, w_in[0], w_out[0]))
    attn_parts, grad_near, first_own, second_own = tied
    attn_turned = [attn_parts[0]] + [shift(attn_parts[r], r) for r in range(1, n)]
    attn_turned = [unpack_rows(a) for a in attn_turned]
    attn_rows = jnp.concatenate(attn_turned, axis=1)

    pair = [(i, i ^ 1) for i in range(n)]
    first_other = lax.ppermute(first_own, "ctx", pair)
    second_other = lax.ppermute(second_own, "ctx", pair)
    grad_far = shift(grad_near, n // 2)

    resid = row_data + dot_nn(attn_rows, w_turned)
    scale_two = norm_scale(resid)
    normed_two = (resid * scale_two * gain_ffn).astype(bfloat)
    sent = dot_tn(dispatch_mat, normed_two).astype(bfloat)
    near = to_plane(sent.reshape(experts, capacity, model_width)).reshape(slots, model_width)
    far = shift(near, n // 2)

    def expert(rows, grad_rows):
        logits = dot_nn(rows, w_router)
        probs = jax.nn.softmax(logits, axis=-1)
        hot = (jnp.arange(experts) == spot).astype(single)[None, :]
        gate = jnp.sum(probs * hot, axis=-1, keepdims=True)
        scaled = (gate * grad_rows.astype(single)).astype(bfloat)
        made, back, hidden_parts, pre_parts = 0.0, 0.0, [], []
        grad_gate = 0.0
        for first, second in ((first_own, second_own), (first_other, second_other)):
            pre = dot_nn(rows, first)
            normal = 0.5 * (1.0 + lax.erf(pre * (0.5**0.5)))
            density = jnp.exp(-0.5 * pre * pre) * 0.3989422804014327
            hidden = pre * normal
            pull = dot_nt(grad_rows, second)
            grad_gate = grad_gate + jnp.sum(hidden * pull, axis=-1, keepdims=True)
            grad_pre = (gate * pull * (normal + pre * density)).astype(bfloat)
            hidden = hidden.astype(bfloat)
            made = made + dot_nn(hidden, second)
            back = back + dot_nt(grad_pre, first)
            hidden_parts.append(hidden)
            pre_parts.append(grad_pre)
        grad_logits = (grad_gate * probs * (hot - gate)).astype(bfloat)
        back = back + dot_nt(grad_logits, w_router)
        return made, back, hidden_parts, pre_parts, grad_logits, scaled

    near_made, near_back, near_hidden, near_pre, near_logits, near_scaled = expert(near, grad_near)
    far_made, far_back, far_hidden, far_pre, far_logits, far_scaled = expert(far, grad_far)
    back_sum = near_back + shift(far_back.astype(bfloat), n // 2).astype(single)
    back_home = to_plane(back_sum.astype(bfloat).reshape(experts, capacity, model_width))
    made_sum = near_made + shift(far_made.astype(bfloat), n // 2).astype(single)
    made_home = to_plane(made_sum.astype(bfloat).reshape(experts, capacity, model_width))

    rows_two = jnp.concatenate([near, far], axis=0)
    scaled_two = jnp.concatenate([near_scaled, far_scaled], axis=0)
    hidden_two = [jnp.concatenate(p, axis=0) for p in zip(near_hidden, far_hidden)]
    pre_two = [jnp.concatenate(p, axis=0) for p in zip(near_pre, far_pre)]
    logits_two = jnp.concatenate([near_logits, far_logits], axis=0)
    first_sent = lax.ppermute(dot_tn(rows_two, pre_two[1]).astype(bfloat), "ctx", pair)
    second_sent = lax.ppermute(dot_tn(hidden_two[1], scaled_two).astype(bfloat), "ctx", pair)
    grad_first = dot_tn(rows_two, pre_two[0]) + first_sent.astype(single)
    grad_second = dot_tn(hidden_two[0], scaled_two) + second_sent.astype(single)
    grad_router = dot_tn(rows_two, logits_two)

    grad_normed_two = dot_nn(dispatch_mat, back_home.reshape(slots, model_width))
    grad_gain_ffn = jnp.sum(grad_normed_two * resid * scale_two, axis=0)
    grad_resid = grad_in + norm_back(grad_normed_two, resid, scale_two, gain_ffn)
    grad_branch = grad_resid.astype(bfloat)
    grad_attn = dot_nt(grad_branch, w_turned).astype(bfloat)
    attn_grads = [
        pack_rows(grad_attn[:, r * width : (r + 1) * width]) for r in range(n)
    ]
    attn_grads = [attn_grads[0]] + [shift(attn_grads[r], n - r) for r in range(1, n)]

    grad_output = dot_tn(attn_rows, grad_branch).astype(bfloat).reshape(n, width, model_width)
    slices = [grad_output[0]] + [shift(grad_output[r], n - r) for r in range(1, n)]
    output_slice = sum(s.astype(single) for s in slices)
    output_all = gather_output(sum_plane(output_slice))

    gate = jnp.sum(
        jax.nn.softmax(dot_nn(normed_two, w_router), axis=-1) * route_hot.astype(single), axis=-1
    )
    picked = dot_nn(dispatch_mat, made_home.reshape(slots, model_width))
    layer_out = resid + gate[:, None] * picked

    grad_qkv, parts, grad_gain_part, grad_rel = attend_back(
        place_in, attn_grads, qkv, lse, rel, w_local, normed_all, gain_attn.reshape(1, -1), heads
    )
    table_part = lax.dot_general(
        bucket_hot, grad_rel[:, :-1], (((0,), (1,)), ((), ())), precision=exact_prec
    )
    extra = jnp.concatenate(
        [
            grad_gain_part.reshape(model_width, 1),
            grad_gain_ffn.reshape(model_width, 1),
            jnp.pad(table_part, ((0, model_width - NB), (0, 0))),
            grad_router,
        ],
        axis=1,
    )
    extra = jnp.pad(extra, ((0, 0), (0, -(3 * width + extra.shape[1]) % 128)))
    late = jnp.concatenate([dot_tn(normed_all, grad_qkv), extra], axis=1)
    grads = gather_late(sum_plane(late), width, model_width)
    parts_in = [parts[0]] + [shift(parts[r], r) for r in range(1, n)]
    grad_normed_one = sum(p.astype(single) for p in parts_in)
    scale_one = norm_scale(row_data)
    grad_tokens = grad_resid + norm_back(grad_normed_one, row_data, scale_one, gain_attn)

    extra = grads[3]
    totals = jnp.sum(extra, axis=0)
    grad_gain_attn = totals[:, 0]
    grad_gain_ffn = totals[:, 1]
    grad_table = extra[:, :NB, 2 : 2 + heads].transpose(1, 0, 2).reshape(NB, H)
    grad_router = totals[:, 2 + heads : 2 + heads + experts]
    return (
        layer_out.reshape(seq_dev, block_len, model_width).astype(bfloat),
        grad_tokens.reshape(seq_dev, block_len, model_width).astype(bfloat),
        grad_gain_attn,
        grads[0],
        grads[1],
        grads[2],
        output_all,
        grad_table,
        grad_gain_ffn,
        grad_router,
        grad_first[None],
        grad_second[None],
    )


def solution(mesh):
    spread = P(("dp", "expert"), "ctx", None)
    first = P(("dp", "expert"), None, "ctx")
    return jax.shard_map(
        shards,
        mesh=mesh,
        in_specs=(spread,) * 3 + (P(),) * 9 + (first, spread),
        out_specs=(spread,) * 2 + (P(),) * 8 + (first, spread),
        check_vma=False,
    )
```

time: 825 us -> 424 us (0.51)
  waiting for transfers between devices: 381 us -> 175 us
  local copies, waits for them, and re-layouts: 181 us -> 21.5 us
  starting transfers between devices: 18.1 us -> 100 us
  matrix products: 126 us -> 57.7 us
  Pallas kernels: 0 us -> 44.1 us
  blocking collectives: 44.1 us -> 0 us
  other arithmetic: 51.3 us -> 15.4 us
  between operations: 14.7 us -> 2.22 us
    psum x1 -> x0, waiting for transfers between devices: 196 us -> none  [shards(): lax.psum((grad_gain_attn, grad_query_w, grad_key_w, grad_value_w, grad_ou...]
    ppermute x0 -> x43, waiting for transfers between devices: none -> 169 us  [the longest x25 151 us: shift(): return lax.ppermute(block, 'ctx', [(i, (i + by) % n) for i in range(n)])]
    reshape x4 -> x3, local copies, waits for them, and re-layouts: 113 us -> 1.78 us  [the longest x1 0.62 us: shards(): grad_table = extra[:, :NB, 2:2 + heads].transpose(1, 0, 2).reshape(NB, H)]
    all_gather x4 -> x0, waiting for transfers between devices: 107 us -> none  [the longest x1 75.7 us: shards(): lax.all_gather(w_out, 'ctx', axis=1, tiled=True)]
    ppermute x0 -> x43, starting transfers between devices: none -> 76.2 us  [the longest x25 64.1 us: shift(): return lax.ppermute(block, 'ctx', [(i, (i + by) % n) for i in range(n)])]
    reduce_scatter x4 -> x0, waiting for transfers between devices: 70.8 us -> none  [the longest x1 65.9 us: shards(): lax.psum_scatter(full_second[None].astype(jnp.bfloat16), 'ctx', scatter_d...]
    dot_general x34 -> x37, matrix products: 126 us -> 57.7 us  [the longest x9 24.2 us: dot_tn(): lax.dot_general(left, right, (((0,), (0,)), ((), ())), preferred_element_...]
    pallas_call x0 -> x4, Pallas kernels: none -> 44.1 us  [the longest x1 22.7 us: attend_back(): pl.pallas_call(functools.partial(attend_back_kernel, n, heads), out_shape...]
  transfers between devices with their start and end apart: 13 -> 49, of which waited for: 7 -> 18; matrix products, arithmetic and copies ran while one was open for 35% -> 17% of each run, Pallas kernels for 0% -> 9%
where the time goes in v2:
time: 424 us; the launch traced here: 417 us
  waiting for transfers between devices  175 us (41%)
  starting transfers between devices  100 us (24%)
  matrix products  57.7 us (14%)
  Pallas kernels  44.1 us (10%)
  local copies, waits for them, and re-layouts  21.5 us (5%)
  other arithmetic  15.4 us (4%)
    ppermute x25, waiting for transfers between devices, shift(): return lax.ppermute(block, 'ctx', [(i, (i + by) % n) for i in range(n)])  151 us
    ppermute x25, starting transfers between devices, shift(): return lax.ppermute(block, 'ctx', [(i, (i + by) % n) for i in range(n)])  64.1 us
    dot_general x9, matrix products, dot_tn(): lax.dot_general(left, right, (((0,), (0,)), ((), ())), preferred_element_...  24.2 us
    all_to_all x6, starting transfers between devices, to_plane(): lax.all_to_all(blocks, PLANE, split_axis=0, concat_axis=0, tiled=True)  24.1 us
    pallas_call x1, Pallas kernels, attend_back(): pl.pallas_call(functools.partial(attend_back_kernel, n, heads), out_shape...  22.7 us
    ppermute x14, waiting for transfers between devices, swap_plane(): return lax.ppermute(block, PLANE, [(i, i ^ mask) for i in range(count)])  17.6 us
    dot_general x15, matrix products, dot_nn(): lax.dot_general(left, right, (((1,), (0,)), ((), ())), preferred_element_...  17.1 us
    dot_general x11, matrix products, dot_nt(): lax.dot_general(left, right, (((1,), (1,)), ((), ())), preferred_element_...  13.8 us
  transfers between devices with their start and end apart: 49, of which 18 were waited for; matrix products, arithmetic and copies ran while one was open for 17% of the time, Pallas kernels for 9%

profile of v2, /device:TPU:0, one launch (start us, length us, event | category | flops | bytes accessed | tf_op | source)
XLA Modules:
  0.0 416.6 jit_solution(17863553382988448838)
XLA Ops:
  0.7 3.1 collective-permute-start
  12.2 3.7 all-to-all-start
  21.8 10.4 %collective-permute-done.1.refs_2_ = bf16[256,768]{1,0:T(8,128)(2,1)} collective-permute-done((bf16[256,768]{1,0:T(8,128)(2,1)}, bf16[256,768]{1,0:T(8,128)(2,1)}, u32[]{:S(2)}, u32[]{:S(2)}) %collective-permute-start.1) | collective-permute-done | bytes 393248 | tf_op jit(solution)/shard_map/ppermute | solution.py:226
  32.2 12.0 %attend.1 = (bf16[1024,768]{1,0:T(8,128)(2,1)}, bf16[1024,576]{1,0:T(8,128)(2,1)}, f32[1024,128]{1,0:T(8,128)}, bf16[4,128,384]{2,1,0:T(8,128)(2,1)}) custom-call(s32[1]{0:T(128)} %bitcast.1.place_ref, bf16[256,768]{1,0:T(8,128)(2,1)} %bitcast.129, bf16[256,768]{1,0:T(8,128)(2,1)} %copy-done.81, bf16[256,768]{1,0:T(8,128)(2,1)} %collective-permute-done.1.refs_2_, ...), custom_call_target="tpu_custom_call" | custom-call | flops 1711276032 | bytes 6291456 | tf_op jit(solution)/shard_map/attend/pallas_call | solution.py:117
  45.5 10.0 %collective-permute-start.5 = (bf16[128,384]{1,0:T(8,128)(2,1)S(1)}, bf16[128,384]{1,0:T(8,128)(2,1)S(1)}, u32[]{:S(2)}, u32[]{:S(2)}) collective-permute-start(bf16[128,384]{1,0:T(8,128)(2,1)S(1)} %get-tuple-element.107), channel_id=1, source_target_pairs={{0,6},{2,0},{4,2},{6,4},{1,7},{3,1},{5,3},{7,5},{8,14},{10,8},{12,... | collective-permute-start | bytes 294920 | tf_op jit(solution)/shard_map/ppermute | solution.py:226
  58.8 6.2 %collective-permute-done.4 = bf16[128,384]{1,0:T(8,128)(2,1)S(1)} collective-permute-done((bf16[128,384]{1,0:T(8,128)(2,1)S(1)}, bf16[128,384]{1,0:T(8,128)(2,1)S(1)}, u32[]{:S(2)}, u32[]{:S(2)}) %collective-permute-start.4) | collective-permute-done | bytes 98336 | tf_op jit(solution)/shard_map/ppermute | solution.py:226
  68.9 4.3 %all-to-all-start.1 = ((bf16[8,40,768]{2,1,0:T(8,128)(2,1)}), bf16[8,40,768]{2,1,0:T(8,128)(2,1)}, u32[]{:S(2)}, u32[]{:S(2)}) async-start(bf16[8,40,768]{2,1,0:T(8,128)(2,1)} %bitcast.12), calls=%async_computation.1 | async-start | bytes 983040 | tf_op jit(solution)/shard_map/all_to_all | solution.py:235
  76.3 5.3 %all-to-all-done.1 = bf16[8,40,768]{2,1,0:T(8,128)(2,1)} async-done(((bf16[8,40,768]{2,1,0:T(8,128)(2,1)}), bf16[8,40,768]{2,1,0:T(8,128)(2,1)}, u32[]{:S(2)}, u32[]{:S(2)}) %all-to-all-start.1) | async-done | bytes 491552 | tf_op jit(solution)/shard_map/all_to_all | solution.py:235
  85.2 61.1 %collective-permute-done.8 = bf16[320,768]{1,0:T(8,128)(2,1)S(1)} collective-permute-done((bf16[320,768]{1,0:T(8,128)(2,1)}, bf16[320,768]{1,0:T(8,128)(2,1)S(1)}, u32[]{:S(2)}, u32[]{:S(2)}) %collective-permute-start.8) | collective-permute-done | bytes 491552 | tf_op jit(solution)/shard_map/ppermute | solution.py:226
  149.7 3.2 multiply_reduce_fusion.1
  164.1 3.3 collective-permute-start.11
  170.7 29.9 %collective-permute-done.11 = bf16[320,768]{1,0:T(8,128)(2,1)S(1)} collective-permute-done((bf16[320,768]{1,0:T(8,128)(2,1)S(1)}, bf16[320,768]{1,0:T(8,128)(2,1)S(1)}, u32[]{:S(2)}, u32[]{:S(2)}) %collective-permute-start.11) | collective-permute-done | bytes 491552 | tf_op jit(solution)/shard_map/ppermute | solution.py:226
  201.7 3.9 all-to-all-start.3
  205.6 3.3 convolution_convert_fusion.2
  214.1 4.0 all-to-all-start.2
  229.4 12.4 %collective-permute-done.12.refs_1_ = bf16[128,384]{1,0:T(8,128)(2,1)S(1)} collective-permute-done((bf16[128,384]{1,0:T(8,128)(2,1)S(1)}, bf16[128,384]{1,0:T(8,128)(2,1)S(1)}, u32[]{:S(2)}, u32[]{:S(2)}) %collective-permute-start.12) | collective-permute-done | bytes 98336 | tf_op jit(solution)/shard_map/ppermute | solution.py:226
  244.7 22.7 %attend_back.1 = (bf16[1024,576]{1,0:T(8,128)(2,1)}, bf16[4,256,768]{2,1,0:T(8,128)(2,1)}, f32[1,768]{1,0:T(1,128)}, f32[3,2048]{1,0:T(4,128)}) custom-call(s32[1]{0:T(128)} %bitcast.1.place_ref, bf16[128,384]{1,0:T(8,128)(2,1)} %pad_maximum_fusion.14.refs_0_, bf16[128,384]{1,0:T(8,128)(2,1)} %copy-done.82, bf16[128,384]{1,0:T(8,128)(2,1)} %copy-done.83, ...), custom_call_target="tpu_custom_call" | custom-call | flops 2919235584 | bytes 6291456 | tf_op jit(solution)/shard_map/attend_back/pallas_call | solution.py:197
  267.5 3.4 convolution_convert_fusion.3
  272.9 4.5 %all-to-all-start.5 = ((bf16[8,24,768]{2,1,0:T(8,128)(2,1)}), bf16[8,24,768]{2,1,0:T(8,128)(2,1)}, u32[]{:S(2)}, u32[]{:S(2)}) async-start(bf16[8,24,768]{2,1,0:T(8,128)(2,1)} %bitcast.32), calls=%async_computation.5 | async-start | bytes 589824 | tf_op jit(solution)/shard_map/all_to_all | solution.py:235
  283.9 3.7 all-to-all-start.4
  288.5 3.7 convolution_convert_fusion.1
  294.6 8.2 %collective-permute-start.33 = (bf16[24,768]{1,0:T(8,128)(2,1)S(1)}, bf16[24,768]{1,0:T(8,128)(2,1)S(1)}, u32[]{:S(2)}, u32[]{:S(2)}) collective-permute-start(bf16[24,768]{1,0:T(8,128)(2,1)S(1)} %reduce_sum.195), channel_id=1, source_target_pairs={{0,6},{2,0},{4,2},{6,4},{1,7},{3,1},{5,3},{7,5},{8,14},{10,8},{12,... | collective-permute-start | bytes 110600 | tf_op jit(solution)/shard_map/ppermute | solution.py:226
  306.2 4.3 %collective-permute-start.20 = (bf16[96,640]{1,0:T(8,128)(2,1)}, bf16[96,640]{1,0:T(8,128)(2,1)S(1)}, u32[]{:S(2)}, u32[]{:S(2)}) collective-permute-start(bf16[96,640]{1,0:T(8,128)(2,1)} %reduce_sum.193), channel_id=1, source_target_pairs={{0,6},{2,0},{4,2},{6,4},{1,7},{3,1},{5,3},{7,5},{8,14},{10,8},{12,... | collective-permute-start | bytes 368648 | tf_op jit(solution)/shard_map/ppermute | solution.py:226
  311.9 10.8 %collective-permute-done.33 = bf16[24,768]{1,0:T(8,128)(2,1)S(1)} collective-permute-done((bf16[24,768]{1,0:T(8,128)(2,1)S(1)}, bf16[24,768]{1,0:T(8,128)(2,1)S(1)}, u32[]{:S(2)}, u32[]{:S(2)}) %collective-permute-start.33) | collective-permute-done | bytes 36896 | tf_op jit(solution)/shard_map/ppermute | solution.py:226
  322.7 5.1 %collective-permute-start.17 = (bf16[256,768]{1,0:T(8,128)(2,1)S(1)}, bf16[256,768]{1,0:T(8,128)(2,1)S(1)}, u32[]{:S(2)}, u32[]{:S(2)}) collective-permute-start(bf16[256,768]{1,0:T(8,128)(2,1)S(1)} %get-tuple-element.85), channel_id=1, source_target_pairs={{0,6},{2,0},{4,2},{6,4},{1,7},{3,1},{5,3},{7,5},{8,14},{10,8},{12,... | collective-permute-start | bytes 1179656 | tf_op jit(solution)/shard_map/ppermute | solution.py:226
  330.0 10.7 %collective-permute-start.19 = (bf16[96,640]{1,0:T(8,128)(2,1)}, bf16[96,640]{1,0:T(8,128)(2,1)S(1)}, u32[]{:S(2)}, u32[]{:S(2)}) collective-permute-start(bf16[96,640]{1,0:T(8,128)(2,1)} %reduce_sum.193), channel_id=1, source_target_pairs={{0,4},{2,6},{4,0},{6,2},{1,5},{3,7},{5,1},{7,3},{8,12},{10,14},{12... | collective-permute-start | bytes 368648 | tf_op jit(solution)/shard_map/ppermute | solution.py:226
  343.3 4.0 add_bitcast_fusion.1
  348.2 14.7 %collective-permute-done.19 = bf16[96,640]{1,0:T(8,128)(2,1)S(1)} collective-permute-done((bf16[96,640]{1,0:T(8,128)(2,1)}, bf16[96,640]{1,0:T(8,128)(2,1)S(1)}, u32[]{:S(2)}, u32[]{:S(2)}) %collective-permute-start.19) | collective-permute-done | bytes 122912 | tf_op jit(solution)/shard_map/ppermute | solution.py:226
  369.2 3.8 add_bitcast_fusion
  378.7 14.6 %collective-permute-done.37.refs_4_ = bf16[4,24,768]{2,1,0:T(8,128)(2,1)S(1)} collective-permute-done((bf16[4,24,768]{2,1,0:T(8,128)(2,1)S(1)}, bf16[4,24,768]{2,1,0:T(8,128)(2,1)S(1)}, u32[]{:S(2)}, u32[]{:S(2)}) %collective-permute-start.37) | collective-permute-done | bytes 147488 | tf_op jit(solution)/shard_map/ppermute | solution.py:231
  399.7 3.0 placed.3
  404.6 6.4 %placed.2 = (f32[768,768]{1,0:T(8,128)}, f32[768,768]{1,0:T(8,128)}, f32[768,768]{1,0:T(8,128)}, f32[4,768,64]{2,1,0:T(8,128)}) custom-call(s32[2]{0:T(128)} %pad_add_fusion.spot_ref, bf16[4,96,640]{2,1,0:T(8,128)(2,1)} %copy-done.10, bf16[4,96,640]{2,1,0:T(8,128)(2,1)} %copy-done.28, bf16[4,96,640]{2,1,0:T(8,128)(2,1)} %copy-done.31, ...), custom_call_target="tpu_custom_call" | custom-call | bytes 12000000 | tf_op jit(solution)/shard_map/placed/pallas_call | solution.py:284
  (345 shorter events, 114.7 us)
Async XLA Ops:
  0.7 21.1 %collective-permute-start = (bf16[256,768]{1,0:T(8,128)(2,1)}, bf16[256,768]{1,0:T(8,128)(2,1)S(1)}, u32[]{:S(2)}, u32[]{:S(2)}) collective-permute-start(bf16[256,768]{1,0:T(8,128)(2,1)} %bitcast.126), channel_id=1, source_target_pairs={{0,2},{2,4},{4,6},{6,0},{1,3},{3,5},{5,7},{7,1},{8,10},{10,12},{12... | collective-permute-start | bytes 1179656 | tf_op jit(solution)/shard_map/ppermute | solution.py:226
  3.8 28.4 %collective-permute-start.1 = (bf16[256,768]{1,0:T(8,128)(2,1)}, bf16[256,768]{1,0:T(8,128)(2,1)}, u32[]{:S(2)}, u32[]{:S(2)}) collective-permute-start(bf16[256,768]{1,0:T(8,128)(2,1)} %bitcast.127), channel_id=1, source_target_pairs={{0,4},{2,6},{4,0},{6,2},{1,5},{3,7},{5,1},{7,3},{8,12},{10,14},{12... | collective-permute-start | bytes 1179656 | tf_op jit(solution)/shard_map/ppermute | solution.py:226
  6.3 25.9 %collective-permute-start.2 = (bf16[256,768]{1,0:T(8,128)(2,1)}, bf16[256,768]{1,0:T(8,128)(2,1)}, u32[]{:S(2)}, u32[]{:S(2)}) collective-permute-start(bf16[256,768]{1,0:T(8,128)(2,1)} %bitcast.128), channel_id=1, source_target_pairs={{0,6},{2,0},{4,2},{6,4},{1,7},{3,1},{5,3},{7,5},{8,14},{10,8},{12,... | collective-permute-start | bytes 1179656 | tf_op jit(solution)/shard_map/ppermute | solution.py:226
  12.2 32.0 %all-to-all-start = ((bf16[8,40,768]{2,1,0:T(8,128)(2,1)}), bf16[8,40,768]{2,1,0:T(8,128)(2,1)S(1)}, u32[]{:S(2)}, u32[]{:S(2)}) async-start(bf16[8,40,768]{2,1,0:T(8,128)(2,1)} %bitcast.4), calls=%async_computation | async-start | bytes 983040 | tf_op jit(solution)/shard_map/all_to_all | solution.py:235
  73.7 82.5 %collective-permute-start.6 = (bf16[768,768]{1,0:T(8,128)(2,1)S(1)}, bf16[768,768]{1,0:T(8,128)(2,1)S(1)}, u32[]{:S(2)}, u32[]{:S(2)}) collective-permute-start(bf16[768,768]{1,0:T(8,128)(2,1)S(1)} %bitcast.113), channel_id=1, source_target_pairs={{0,2},{2,0},{4,6},{6,4},{1,3},{3,1},{5,7},{7,5},{8,10},{10,8},{12,... | collective-permute-start | bytes 3538952 | tf_op jit(solution)/shard_map/ppermute | solution.py:395
  73.7 83.0 %collective-permute-start.7 = (bf16[768,768]{1,0:T(8,128)(2,1)}, bf16[768,768]{1,0:T(8,128)(2,1)}, u32[]{:S(2)}, u32[]{:S(2)}) collective-permute-start(bf16[768,768]{1,0:T(8,128)(2,1)} %bitcast.118), channel_id=1, source_target_pairs={{0,2},{2,0},{4,6},{6,4},{1,3},{3,1},{5,7},{7,5},{8,10},{10,8},{12,... | collective-permute-start | bytes 3538952 | tf_op jit(solution)/shard_map/ppermute | solution.py:396
  75.7 73.9 %collective-permute-start.10 = (bf16[320,768]{1,0:T(8,128)(2,1)}, bf16[320,768]{1,0:T(8,128)(2,1)}, u32[]{:S(2)}, u32[]{:S(2)}) collective-permute-start(bf16[320,768]{1,0:T(8,128)(2,1)} %bitcast.131), channel_id=1, source_target_pairs={{0,4},{2,6},{4,0},{6,2},{1,5},{3,7},{5,1},{7,3},{8,12},{10,14},{12... | collective-permute-start | bytes 1474568 | tf_op jit(solution)/shard_map/ppermute | solution.py:226
  81.7 64.6 %collective-permute-start.8 = (bf16[320,768]{1,0:T(8,128)(2,1)}, bf16[320,768]{1,0:T(8,128)(2,1)S(1)}, u32[]{:S(2)}, u32[]{:S(2)}) collective-permute-start(bf16[320,768]{1,0:T(8,128)(2,1)} %bitcast.13), channel_id=1, source_target_pairs={{0,4},{2,6},{4,0},{6,2},{1,5},{3,7},{5,1},{7,3},{8,12},{10,14},{12... | collective-permute-start | bytes 1474568 | tf_op jit(solution)/shard_map/ppermute | solution.py:226
  164.1 36.4 %collective-permute-start.11 = (bf16[320,768]{1,0:T(8,128)(2,1)S(1)}, bf16[320,768]{1,0:T(8,128)(2,1)S(1)}, u32[]{:S(2)}, u32[]{:S(2)}) collective-permute-start(bf16[320,768]{1,0:T(8,128)(2,1)S(1)} %fusion.4), channel_id=1, source_target_pairs={{0,4},{2,6},{4,0},{6,2},{1,5},{3,7},{5,1},{7,3},{8,12},{10,14},{12... | collective-permute-start | bytes 1474568 | tf_op jit(solution)/shard_map/ppermute | solution.py:226
  170.1 40.8 %collective-permute-start.9 = (bf16[320,768]{1,0:T(8,128)(2,1)}, bf16[320,768]{1,0:T(8,128)(2,1)}, u32[]{:S(2)}, u32[]{:S(2)}) collective-permute-start(bf16[320,768]{1,0:T(8,128)(2,1)} %fusion.2), channel_id=1, source_target_pairs={{0,4},{2,6},{4,0},{6,2},{1,5},{3,7},{5,1},{7,3},{8,12},{10,14},{12... | collective-permute-start | bytes 1474568 | tf_op jit(solution)/shard_map/ppermute | solution.py:226
  208.9 97.2 %collective-permute-start.41 = (bf16[768,768]{1,0:T(8,128)(2,1)}, bf16[768,768]{1,0:T(8,128)(2,1)}, u32[]{:S(2)}, u32[]{:S(2)}) collective-permute-start(bf16[768,768]{1,0:T(8,128)(2,1)} %convolution_convert_fusion.2), channel_id=1, source_target_pairs={{0,2},{2,0},{4,6},{6,4},{1,3},{3,1},{5,7},{7,5},{8,10},{10,8},{12,... | collective-permute-start | bytes 3538952 | tf_op jit(solution)/shard_map/ppermute | solution.py:443
  214.1 58.8 %all-to-all-start.2 = ((bf16[8,40,768]{2,1,0:T(8,128)(2,1)}), bf16[8,40,768]{2,1,0:T(8,128)(2,1)S(1)}, u32[]{:S(2)}, u32[]{:S(2)}) async-start(bf16[8,40,768]{2,1,0:T(8,128)(2,1)} %bitcast.14), calls=%async_computation.2 | async-start | bytes 983040 | tf_op jit(solution)/shard_map/all_to_all | solution.py:235
  222.3 19.5 %collective-permute-start.12 = (bf16[128,384]{1,0:T(8,128)(2,1)S(1)}, bf16[128,384]{1,0:T(8,128)(2,1)S(1)}, u32[]{:S(2)}, u32[]{:S(2)}) collective-permute-start(bf16[128,384]{1,0:T(8,128)(2,1)S(1)} %pad_maximum_fusion.15), channel_id=1, source_target_pairs={{0,6},{2,0},{4,2},{6,4},{1,7},{3,1},{5,3},{7,5},{8,14},{10,8},{12,... | collective-permute-start | bytes 294920 | tf_op jit(solution)/shard_map/ppermute | solution.py:226
  226.0 18.0 %collective-permute-start.14 = (bf16[128,384]{1,0:T(8,128)(2,1)S(1)}, bf16[128,384]{1,0:T(8,128)(2,1)S(1)}, u32[]{:S(2)}, u32[]{:S(2)}) collective-permute-start(bf16[128,384]{1,0:T(8,128)(2,1)S(1)} %pad_maximum_fusion.17), channel_id=1, source_target_pairs={{0,2},{2,4},{4,6},{6,0},{1,3},{3,5},{5,7},{7,1},{8,10},{10,12},{12... | collective-permute-start | bytes 294920 | tf_op jit(solution)/shard_map/ppermute | solution.py:226
  227.7 44.4 %collective-permute-start.30 = (bf16[192,768]{1,0:T(8,128)(2,1)S(1)}, bf16[192,768]{1,0:T(8,128)(2,1)S(1)}, u32[]{:S(2)}, u32[]{:S(2)}) collective-permute-start(bf16[192,768]{1,0:T(8,128)(2,1)S(1)} %get-tuple-element.88), channel_id=1, source_target_pairs={{0,2},{2,4},{4,6},{6,0},{1,3},{3,5},{5,7},{7,1},{8,10},{10,12},{12... | collective-permute-start | bytes 884744 | tf_op jit(solution)/shard_map/ppermute | solution.py:226
  241.8 30.2 %collective-permute-start.29 = (bf16[192,768]{1,0:T(8,128)(2,1)S(1)}, bf16[192,768]{1,0:T(8,128)(2,1)S(1)}, u32[]{:S(2)}, u32[]{:S(2)}) collective-permute-start(bf16[192,768]{1,0:T(8,128)(2,1)S(1)} %get-tuple-element.89), channel_id=1, source_target_pairs={{0,4},{2,6},{4,0},{6,2},{1,5},{3,7},{5,1},{7,3},{8,12},{10,14},{12... | collective-permute-start | bytes 884744 | tf_op jit(solution)/shard_map/ppermute | solution.py:226
  241.8 30.2 %collective-permute-start.28 = (bf16[192,768]{1,0:T(8,128)(2,1)S(1)}, bf16[192,768]{1,0:T(8,128)(2,1)S(1)}, u32[]{:S(2)}, u32[]{:S(2)}) collective-permute-start(bf16[192,768]{1,0:T(8,128)(2,1)S(1)} %get-tuple-element.87), channel_id=1, source_target_pairs={{0,6},{2,0},{4,2},{6,4},{1,7},{3,1},{5,3},{7,5},{8,14},{10,8},{12,... | collective-permute-start | bytes 884744 | tf_op jit(solution)/shard_map/ppermute | solution.py:226
  283.9 21.5 %all-to-all-start.4 = ((bf16[8,96,640]{2,1,0:T(8,128)(2,1)}), bf16[8,96,640]{2,1,0:T(8,128)(2,1)S(1)}, u32[]{:S(2)}, u32[]{:S(2)}) async-start(bf16[8,96,640]{2,1,0:T(8,128)(2,1)} %pad_maximum_fusion.3), calls=%async_computation.4 | async-start | bytes 1966080 | tf_op jit(solution)/shard_map/all_to_all | solution.py:235
  292.1 73.4 %collective-permute-start.42 = (bf16[768,768]{1,0:T(8,128)(2,1)}, bf16[768,768]{1,0:T(8,128)(2,1)}, u32[]{:S(2)}, u32[]{:S(2)}) collective-permute-start(bf16[768,768]{1,0:T(8,128)(2,1)} %convolution_convert_fusion.1), channel_id=1, source_target_pairs={{0,2},{2,0},{4,6},{6,4},{1,3},{3,1},{5,7},{7,5},{8,10},{10,8},{12,... | collective-permute-start | bytes 3538952 | tf_op jit(solution)/shard_map/ppermute | solution.py:444
  294.6 28.1 %collective-permute-start.33 = (bf16[24,768]{1,0:T(8,128)(2,1)S(1)}, bf16[24,768]{1,0:T(8,128)(2,1)S(1)}, u32[]{:S(2)}, u32[]{:S(2)}) collective-permute-start(bf16[24,768]{1,0:T(8,128)(2,1)S(1)} %reduce_sum.195), channel_id=1, source_target_pairs={{0,6},{2,0},{4,2},{6,4},{1,7},{3,1},{5,3},{7,5},{8,14},{10,8},{12,... | collective-permute-start | bytes 110600 | tf_op jit(solution)/shard_map/ppermute | solution.py:226
  302.8 25.1 %collective-permute-start.32 = (bf16[24,768]{1,0:T(8,128)(2,1)S(1)}, bf16[24,768]{1,0:T(8,128)(2,1)S(1)}, u32[]{:S(2)}, u32[]{:S(2)}) collective-permute-start(bf16[24,768]{1,0:T(8,128)(2,1)S(1)} %reduce_sum.195), channel_id=1, source_target_pairs={{0,4},{2,6},{4,0},{6,2},{1,5},{3,7},{5,1},{7,3},{8,12},{10,14},{12... | collective-permute-start | bytes 110600 | tf_op jit(solution)/shard_map/ppermute | solution.py:226
  303.4 26.6 %collective-permute-start.31 = (bf16[24,768]{1,0:T(8,128)(2,1)S(1)}, bf16[24,768]{1,0:T(8,128)(2,1)}, u32[]{:S(2)}, u32[]{:S(2)}) collective-permute-start(bf16[24,768]{1,0:T(8,128)(2,1)S(1)} %reduce_sum.195), channel_id=1, source_target_pairs={{0,2},{2,4},{4,6},{6,0},{1,3},{3,5},{5,7},{7,1},{8,10},{10,12},{12... | collective-permute-start | bytes 110600 | tf_op jit(solution)/shard_map/ppermute | solution.py:226
  306.2 34.5 %collective-permute-start.20 = (bf16[96,640]{1,0:T(8,128)(2,1)}, bf16[96,640]{1,0:T(8,128)(2,1)S(1)}, u32[]{:S(2)}, u32[]{:S(2)}) collective-permute-start(bf16[96,640]{1,0:T(8,128)(2,1)} %reduce_sum.193), channel_id=1, source_target_pairs={{0,6},{2,0},{4,2},{6,4},{1,7},{3,1},{5,3},{7,5},{8,14},{10,8},{12,... | collective-permute-start | bytes 368648 | tf_op jit(solution)/shard_map/ppermute | solution.py:226
  322.7 43.3 %collective-permute-start.17 = (bf16[256,768]{1,0:T(8,128)(2,1)S(1)}, bf16[256,768]{1,0:T(8,128)(2,1)S(1)}, u32[]{:S(2)}, u32[]{:S(2)}) collective-permute-start(bf16[256,768]{1,0:T(8,128)(2,1)S(1)} %get-tuple-element.85), channel_id=1, source_target_pairs={{0,6},{2,0},{4,2},{6,4},{1,7},{3,1},{5,3},{7,5},{8,14},{10,8},{12,... | collective-permute-start | bytes 1179656 | tf_op jit(solution)/shard_map/ppermute | solution.py:226
  327.8 39.9 %collective-permute-start.16 = (bf16[256,768]{1,0:T(8,128)(2,1)S(1)}, bf16[256,768]{1,0:T(8,128)(2,1)S(1)}, u32[]{:S(2)}, u32[]{:S(2)}) collective-permute-start(bf16[256,768]{1,0:T(8,128)(2,1)S(1)} %get-tuple-element.86), channel_id=1, source_target_pairs={{0,4},{2,6},{4,0},{6,2},{1,5},{3,7},{5,1},{7,3},{8,12},{10,14},{12... | collective-permute-start | bytes 1179656 | tf_op jit(solution)/shard_map/ppermute | solution.py:226
  330.0 32.9 %collective-permute-start.19 = (bf16[96,640]{1,0:T(8,128)(2,1)}, bf16[96,640]{1,0:T(8,128)(2,1)S(1)}, u32[]{:S(2)}, u32[]{:S(2)}) collective-permute-start(bf16[96,640]{1,0:T(8,128)(2,1)} %reduce_sum.193), channel_id=1, source_target_pairs={{0,4},{2,6},{4,0},{6,2},{1,5},{3,7},{5,1},{7,3},{8,12},{10,14},{12... | collective-permute-start | bytes 368648 | tf_op jit(solution)/shard_map/ppermute | solution.py:226
  340.7 22.2 %collective-permute-start.18 = (bf16[96,640]{1,0:T(8,128)(2,1)}, bf16[96,640]{1,0:T(8,128)(2,1)S(1)}, u32[]{:S(2)}, u32[]{:S(2)}) collective-permute-start(bf16[96,640]{1,0:T(8,128)(2,1)} %reduce_sum.193), channel_id=1, source_target_pairs={{0,2},{2,4},{4,6},{6,0},{1,3},{3,5},{5,7},{7,1},{8,10},{10,12},{12... | collective-permute-start | bytes 368648 | tf_op jit(solution)/shard_map/ppermute | solution.py:226
  365.6 30.6 %collective-permute-start.21 = (bf16[4,96,640]{2,1,0:T(8,128)(2,1)S(1)}, bf16[4,96,640]{2,1,0:T(8,128)(2,1)S(1)}, u32[]{:S(2)}, u32[]{:S(2)}) collective-permute-start(bf16[4,96,640]{2,1,0:T(8,128)(2,1)S(1)} %pad_maximum_fusion.7.refs_0_), channel_id=1, source_target_pairs={{0,1},{1,0},{8,9},{9,8},{16,17},{17,16},{24,25},{25,24},{2,3},{3,2... | collective-permute-start | bytes 1474568 | tf_op jit(solution)/shard_map/ppermute | solution.py:231
  366.0 30.3 %collective-permute-start.24 = (bf16[4,96,640]{2,1,0:T(8,128)(2,1)S(1)}, bf16[4,96,640]{2,1,0:T(8,128)(2,1)S(1)}, u32[]{:S(2)}, u32[]{:S(2)}) collective-permute-start(bf16[4,96,640]{2,1,0:T(8,128)(2,1)S(1)} %pad_maximum_fusion.7.refs_0_), channel_id=1, source_target_pairs={{0,16},{1,17},{8,24},{9,25},{16,0},{17,1},{24,8},{25,9},{2,18},{3,... | collective-permute-start | bytes 1474568 | tf_op jit(solution)/shard_map/ppermute | solution.py:231
  367.7 29.0 %collective-permute-start.25 = (bf16[4,96,640]{2,1,0:T(8,128)(2,1)S(1)}, bf16[4,96,640]{2,1,0:T(8,128)(2,1)S(1)}, u32[]{:S(2)}, u32[]{:S(2)}) collective-permute-start(bf16[4,96,640]{2,1,0:T(8,128)(2,1)S(1)} %pad_maximum_fusion.7.refs_0_), channel_id=1, source_target_pairs={{0,17},{1,16},{8,25},{9,24},{16,1},{17,0},{24,9},{25,8},{2,19},{3,... | collective-permute-start | bytes 1474568 | tf_op jit(solution)/shard_map/ppermute | solution.py:231
  375.1 18.2 %collective-permute-start.37 = (bf16[4,24,768]{2,1,0:T(8,128)(2,1)S(1)}, bf16[4,24,768]{2,1,0:T(8,128)(2,1)S(1)}, u32[]{:S(2)}, u32[]{:S(2)}) collective-permute-start(bf16[4,24,768]{2,1,0:T(8,128)(2,1)S(1)} %pad_maximum_fusion.13.refs_0_), channel_id=1, source_target_pairs={{0,16},{1,17},{8,24},{9,25},{16,0},{17,1},{24,8},{25,9},{2,18},{3,... | collective-permute-start | bytes 442376 | tf_op jit(solution)/shard_map/ppermute | solution.py:231
  377.0 18.6 %collective-permute-start.38 = (bf16[4,24,768]{2,1,0:T(8,128)(2,1)S(1)}, bf16[4,24,768]{2,1,0:T(8,128)(2,1)S(1)}, u32[]{:S(2)}, u32[]{:S(2)}) collective-permute-start(bf16[4,24,768]{2,1,0:T(8,128)(2,1)S(1)} %pad_maximum_fusion.13.refs_0_), channel_id=1, source_target_pairs={{0,17},{1,16},{8,25},{9,24},{16,1},{17,0},{24,9},{25,8},{2,19},{3,... | collective-permute-start | bytes 442376 | tf_op jit(solution)/shard_map/ppermute | solution.py:231
  (108 other events, 991.5 us)
